TPU v7x, 32 devices: a whole 2x2x4 slice. The times are simulated.
32 devices in a mesh: groups: 2 (over y), expert: 8 (over z, core), dp: 2 (over x).
Axes of the slice: x: 2, y: 2, z: 4, core: 2. Of those that a mesh axis runs over, the one named last changes fastest.
Arguments:
- tokens: bfloat16 [4096, 2048], P(('groups', 'expert', 'dp')), parts along dimension 0, may hold values from -6 to 6
- expert_ids: int32 [4096, 8], P(('groups', 'expert', 'dp')), parts along dimension 0, may hold values from 0 to 15, all different within a row; in each aligned block of 128 rows (0 to 127, 128 to 255, ...) at most 72 rows name the same one
- gate_weights: bfloat16 [4096, 8], P(('groups', 'expert', 'dp')), parts along dimension 0, may hold values from 0.049804688 to 0.5
- cotangent: bfloat16 [4096, 2048], P(('groups', 'expert', 'dp')), parts along dimension 0, may hold values from -0.796875 to 0.796875
- gate_matrix: bfloat16 [16, 2048, 384], P('expert', 'dp'), may hold values from -0.125 to 0.125
- up_weight: bfloat16 [16, 2048, 384], P('expert', 'dp'), may hold values from -0.125 to 0.125
- down_weight: bfloat16 [16, 384, 2048], P('expert', None, 'dp'), may hold values from -0.3125 to 0.3125
Outputs:
- grad_tokens: bfloat16 [4096, 2048], P(('groups', 'expert', 'dp')), parts along dimension 0
- grad_gates: bfloat16 [4096, 8], P(('groups', 'expert', 'dp')), parts along dimension 0
- grad_gate_matrix: bfloat16 [32, 2048, 384], P(('groups', 'expert'), 'dp'), parts along dimension 0
- grad_up: bfloat16 [32, 2048, 384], P(('groups', 'expert'), 'dp'), parts along dimension 0
- grad_down: bfloat16 [32, 384, 2048], P(('groups', 'expert'), None, 'dp'), parts along dimension 0
There are 2 independent parts, one for each index of `groups`. A program takes and returns all parts, laid end to end along the dimension named above; an argument that names none is the same for every part. Nothing has to cross between parts.
Inputs may be any that keep to these rules, and one draw needn't show every extreme that they name: `expert_ids`: each row names 8 different experts; among the 128 tokens of one device no expert is named more than 72 times, and in every draw some expert is named exactly 72 times by the tokens of some device.
All inputs are finite; a program needn't handle non-finite values.
Results may differ from a plain program's by a relative error of at most 0.008.
Values may be sent and summed in bfloat16 or wider, within the bound.
A program may use at most 128 MiB of HBM per device.

v0:
```python
import jax
import jax.numpy as jnp
from jax import lax
from jax.sharding import PartitionSpec as P


def body(tokens, expert_ids, gate_weights, cotangent, gate_matrix, up_weight, down_weight):
    tok_dev, top = expert_ids.shape
    exp_dev = up_weight.shape[0]
    n_peers = lax.axis_size("expert")
    experts = exp_dev * n_peers
    cap = min(tok_dev, tok_dev * top * 9 // (8 * experts))
    width = tokens.shape[1]
    flat_ids = expert_ids.reshape(-1)
    pairs = flat_ids.shape[0]
    onehot = (flat_ids[:, None] == jnp.arange(experts, dtype=jnp.int32)[None, :]).astype(jnp.int32)
    before = jnp.cumsum(onehot, axis=0) - onehot
    position = jnp.sum(before * onehot, axis=1)
    slot = flat_ids * cap + position
    owner = (
        jnp.full((experts * cap,), -1, jnp.int32).at[slot].set(jnp.arange(pairs, dtype=jnp.int32))
    )
    filled = owner >= 0
    safe_pair = jnp.maximum(owner, 0)
    token_row = safe_pair // top
    send_rows = jnp.where(filled[:, None], tokens[token_row], jnp.zeros((), tokens.dtype)).reshape(
        n_peers, exp_dev * cap, width
    )
    send_gate = jnp.where(
        filled, gate_weights.reshape(-1)[safe_pair], jnp.zeros((), gate_weights.dtype)
    ).reshape(n_peers, exp_dev * cap)
    send_grad = jnp.where(
        filled[:, None], cotangent[token_row], jnp.zeros((), cotangent.dtype)
    ).reshape(n_peers, exp_dev * cap, width)
    recv_rows, recv_gate = (
        lax.all_to_all(send_rows, "expert", split_axis=0, concat_axis=0, tiled=True),
        lax.all_to_all(send_gate, "expert", split_axis=0, concat_axis=0, tiled=True),
    )
    full_gate, full_up, full_down = (
        lax.all_gather(gate_matrix, "dp", axis=1, tiled=True),
        lax.all_gather(up_weight, "dp", axis=1, tiled=True),
        lax.all_gather(down_weight, "dp", axis=2, tiled=True),
    )
    rows_four = recv_rows.reshape(n_peers, exp_dev, cap, width)
    pre_gate = jnp.einsum(
        "slcd,ldf->slcf", rows_four, full_gate, preferred_element_type=jnp.float32
    )
    pre_up = jnp.einsum("slcd,ldf->slcf", rows_four, full_up, preferred_element_type=jnp.float32)
    sig = jax.nn.sigmoid(pre_gate)
    active = pre_gate * sig
    hidden = (active * pre_up).astype(jnp.bfloat16)
    recv_grad = lax.all_to_all(send_grad, "expert", split_axis=0, concat_axis=0, tiled=True)
    grad_four = recv_grad.reshape(n_peers, exp_dev, cap, width)
    gate_three = recv_gate.reshape(n_peers, exp_dev, cap).astype(jnp.float32)[..., None]
    back = jnp.einsum("slcd,lfd->slcf", grad_four, full_down, preferred_element_type=jnp.float32)
    gate_grad = jnp.sum(hidden.astype(jnp.float32) * back, axis=3).astype(jnp.bfloat16)
    d_hidden = gate_three * back
    d_gate = (d_hidden * pre_up * (sig * (1.0 + pre_gate * (1.0 - sig)))).astype(jnp.bfloat16)
    d_up = (d_hidden * active).astype(jnp.bfloat16)
    d_out = (gate_three * grad_four.astype(jnp.float32)).astype(jnp.bfloat16)
    both = jnp.einsum("slcf,ldf->slcd", d_gate, full_gate, preferred_element_type=jnp.float32)
    both = both + jnp.einsum("slcf,ldf->slcd", d_up, full_up, preferred_element_type=jnp.float32)
    d_rows = both.astype(jnp.bfloat16)
    ret_rows, ret_gate = (
        lax.all_to_all(
            d_rows.reshape(n_peers, exp_dev * cap, width),
            "expert",
            split_axis=0,
            concat_axis=0,
            tiled=True,
        ),
        lax.all_to_all(
            gate_grad.reshape(n_peers, exp_dev * cap),
            "expert",
            split_axis=0,
            concat_axis=0,
            tiled=True,
        ),
    )
    gate_term = jnp.einsum("slcd,slcf->ldf", rows_four, d_gate, preferred_element_type=jnp.float32)
    up_term = jnp.einsum("slcd,slcf->ldf", rows_four, d_up, preferred_element_type=jnp.float32)
    down_term = jnp.einsum("slcf,slcd->lfd", hidden, d_out, preferred_element_type=jnp.float32)
    gate_sum, up_sum, down_sum = (
        lax.psum_scatter(
            gate_term.astype(jnp.bfloat16), "dp", scatter_dimension=1, tiled=True
        ).astype(jnp.float32),
        lax.psum_scatter(
            up_term.astype(jnp.bfloat16), "dp", scatter_dimension=1, tiled=True
        ).astype(jnp.float32),
        lax.psum_scatter(
            down_term.astype(jnp.bfloat16), "dp", scatter_dimension=2, tiled=True
        ).astype(jnp.float32),
    )
    per_pair = ret_rows.reshape(experts * cap, width)[slot]
    grad_tokens = jnp.sum(per_pair.reshape(tok_dev, top, width).astype(jnp.float32), axis=1).astype(
        jnp.bfloat16
    )
    grad_gates = ret_gate.reshape(-1)[slot].reshape(tok_dev, top)
    return (
        grad_tokens,
        grad_gates,
        gate_sum.astype(jnp.bfloat16),
        up_sum.astype(jnp.bfloat16),
        down_sum.astype(jnp.bfloat16),
    )


def solution(mesh):
    placed = (
        P(("groups", "expert", "dp"), None),
        P(("groups", "expert", "dp"), None),
        P(("groups", "expert", "dp"), None),
        P(("groups", "expert", "dp"), None),
        P("expert", "dp", None),
        P("expert", "dp", None),
        P("expert", None, "dp"),
    )
    return jax.shard_map(
        body,
        mesh=mesh,
        in_specs=placed,
        out_specs=(
            P(("groups", "expert", "dp"), None),
            P(("groups", "expert", "dp"), None),
            P(("groups", "expert"), "dp", None),
            P(("groups", "expert"), "dp", None),
            P(("groups", "expert"), None, "dp"),
        ),
        check_vma=False,
    )
```

profile of v0, /device:TPU:0, one launch (start us, length us, event | category | flops | bytes accessed | tf_op | source)
XLA Modules:
  0.0 445.7 jit_solution(9129793039652720178)
XLA Ops:
  7.2 0.7 broadcast_multiply_fusion
  7.9 0.8 copy.46
  8.9 0.8 copy.50
  10.0 4.5 %reduce-window.6 = s32[16,8,128]{2,1,0:T(8,128)S(1)} reduce-window(s32[16,8,128]{2,1,0:T(8,128)S(1)} %fusion.31, s32[]{:T(128)} %constant.32.clone.1), window={size=1x1x128 pad=0_0x0_0x127_0}, to_apply=%region_0.0 | reduce-window | flops 2080768 | bytes 131076 | tf_op jit(solution)/shard_map/reduce-window
  15.0 4.3 scatter_custom_fusion
  19.4 7.3 %gather_fusion = bf16[1152]{0:T(1024)(128)(2,1)S(1)} fusion(bf16[1024]{0:T(1024)(128)(2,1)S(1)} %reshape.124, s32[2048]{0:T(1024)S(1)} %get-tuple-element.31), kind=kCustom, calls=%fused_computation | custom fusion | bytes 9216 | tf_op jit(solution)/shard_map/gather | solution.py:30
  27.4 6.3 %all-to-all-start = ((bf16[8,1,144]{2,1,0:T(2,128)(2,1)}), bf16[8,1,144]{2,1,0:T(2,128)(2,1)S(1)}, u32[]{:S(2)}, u32[]{:S(2)}) async-start(bf16[8,1,144]{2,1,0:T(2,128)(2,1)} %all_to_all.25), calls=%async_computation | async-start | bytes 16384 | tf_op jit(solution)/shard_map/all_to_all | solution.py:37
  33.8 5.9 %gather_fusion.2 = bf16[1152,2048]{1,0:T(8,128)(2,1)} fusion(bf16[128,2048]{1,0:T(8,128)(2,1)S(1)} %copy-done, s32[2048]{0:T(1024)S(1)} %get-tuple-element.30), kind=kCustom, calls=%fused_computation.2 | custom fusion | bytes 9441792 | tf_op jit(solution)/shard_map/gather | solution.py:26
  39.7 5.9 %gather_fusion.1 = bf16[1152,2048]{1,0:T(8,128)(2,1)} fusion(bf16[128,2048]{1,0:T(8,128)(2,1)S(1)} %copy-done.2, s32[2048]{0:T(1024)S(1)} %get-tuple-element.30), kind=kCustom, calls=%fused_computation.1 | custom fusion | bytes 9441792 | tf_op jit(solution)/shard_map/gather | solution.py:33
  45.7 8.5 %broadcast_select_fusion.1 = (bf16[8,144,2048]{2,1,0:T(8,128)(2,1)}, bf16[8,144,2048]{2,1,0:T(8,128)(2,1)}) fusion(bf16[8,144,2048]{2,1,0:T(8,128)(2,1)} %bitcast.110, pred[8,144]{1,0:T(8,128)(4,1)S(1)} %broadcast_in_dim.42, bf16[8,144,2048]{2,1,0:T(8,128)(2,1)} %bitcast.109), kind=kLoop, calls=%fused_computation.17 | loop fusion | flops 4718592 | bytes 18875520 | tf_op jit(solution)/shard_map/jit(_where)/select_n | solution.py:32
  54.1 5.1 %all-to-all-start.2 = ((bf16[8,144,2048]{2,1,0:T(8,128)(2,1)}), bf16[8,144,2048]{2,1,0:T(8,128)(2,1)}, u32[]{:S(2)}, u32[]{:S(2)}) async-start(bf16[8,144,2048]{2,1,0:T(8,128)(2,1)} %get-tuple-element.29), calls=%async_computation.2 | async-start | bytes 9437184 | tf_op jit(solution)/shard_map/all_to_all | solution.py:36
  60.0 104.6 %all-to-all-done.2 = bf16[8,144,2048]{2,1,0:T(8,128)(2,1)} async-done(((bf16[8,144,2048]{2,1,0:T(8,128)(2,1)}), bf16[8,144,2048]{2,1,0:T(8,128)(2,1)}, u32[]{:S(2)}, u32[]{:S(2)}) %all-to-all-start.2) | async-done | bytes 4718624 | tf_op jit(solution)/shard_map/all_to_all | solution.py:36
  164.6 4.6 %all-to-all-start.1 = ((bf16[8,144,2048]{2,1,0:T(8,128)(2,1)}), bf16[8,144,2048]{2,1,0:T(8,128)(2,1)}, u32[]{:S(2)}, u32[]{:S(2)}) async-start(bf16[8,144,2048]{2,1,0:T(8,128)(2,1)} %get-tuple-element.28), calls=%async_computation.1 | async-start | bytes 9437184 | tf_op jit(solution)/shard_map/all_to_all | solution.py:52
  169.2 0.7 all-gather.6.cloned.1.call-update
  171.0 7.2 %fusion.5 = f32[2,8,72,384]{3,2,1,0:T(8,128)} fusion(bf16[8,2,72,2048]{3,2,1,0:T(8,128)(2,1)} %bitcast.10, bf16[2,2048,384]{2,1,0:T(8,128)(2,1)} %all-gather.8.cloned.1.call-done), kind=kOutput, calls=%fused_computation.19 | convolution fusion | flops 1811939328 | bytes 9633792 | tf_op jit(solution)/shard_map/slcd,ldf->slcf/dot_general | solution.py:45
  178.2 39.7 %all-gather.6.cloned.1.call-done = bf16[2,2048,384]{2,1,0:T(8,128)(2,1)} async-done(((bf16[2,1024,384]{2,1,0:T(8,128)(2,1)}), bf16[2,2048,384]{2,1,0:T(8,128)(2,1)}) %all-gather.6.cloned.1.call-update) | async-done | bytes 3145744 | tf_op jit(solution)/shard_map/all_gather | solution.py:41
  217.9 7.2 %fusion.7 = f32[2,8,72,384]{3,2,1,0:T(8,128)} fusion(bf16[8,2,72,2048]{3,2,1,0:T(8,128)(2,1)} %bitcast.10, bf16[2,2048,384]{2,1,0:T(8,128)(2,1)} %all-gather.6.cloned.1.call-done), kind=kOutput, calls=%fused_computation.21 | convolution fusion | flops 1811939328 | bytes 9633792 | tf_op jit(solution)/shard_map/slcd,ldf->slcf/dot_general | solution.py:48
  225.1 39.3 %all-gather.4.cloned.1.call-done = bf16[2,384,2048]{2,1,0:T(8,128)(2,1)} async-done(((bf16[2,384,1024]{2,1,0:T(8,128)(2,1)}), bf16[2,384,2048]{2,1,0:T(8,128)(2,1)}) %all-gather.4.cloned.1.call-update) | async-done | bytes 3145744 | tf_op jit(solution)/shard_map/all_gather | solution.py:42
  264.4 10.0 %all-to-all-done.1 = bf16[8,144,2048]{2,1,0:T(8,128)(2,1)} async-done(((bf16[8,144,2048]{2,1,0:T(8,128)(2,1)}), bf16[8,144,2048]{2,1,0:T(8,128)(2,1)}, u32[]{:S(2)}, u32[]{:S(2)}) %all-to-all-start.1) | async-done | bytes 4718624 | tf_op jit(solution)/shard_map/all_to_all | solution.py:52
  274.4 7.6 %fusion.25 = (bf16[8,2,72]{2,0,1:T(8,128)(2,1)S(1)}, bf16[8,2,72,384]{3,2,0,1:T(8,128)(2,1)S(1)}, bf16[8,2,72,384]{3,2,0,1:T(8,128)(2,1)S(1)}, bf16[8,2,72,384]{3,2,0,1:T(8,128)(2,1)S(1)}) fusion(f32[2,8,72,384]{3,2,1,0:T(8,128)} %fusion.7, f32[2,8,72,384]{3,2,1,0:T(8,128)} %fusion.5, f32[8,2,72]{2,0,1:T(8,128)S(1)} %copy.52, ...), kind=kOutput, calls=%fused_computation.44 | convolution fusion | flops 1820343168 | bytes 14064384 | tf_op jit(solution)/shard_map/slcd,lfd->slcf/dot_general | solution.py:55
  282.1 6.8 %bitcast_convert_fusion = bf16[2,384,2048]{2,1,0:T(8,128)(2,1)} fusion(bf16[8,2,72,384]{3,2,0,1:T(8,128)(2,1)S(1)} %get-tuple-element.21, bf16[8,2,72,2048]{3,2,1,0:T(8,128)(2,1)} %bitcast.5, f32[8,2,72]{2,1,0:T(2,128)S(1)} %reshape.132), kind=kOutput, calls=%fused_computation.8 | convolution fusion | flops 1820590080 | bytes 8753664 | tf_op jit(solution)/shard_map/slcf,slcd->lfd/dot_general | solution.py:82
  289.1 7.3 %bitcast_convert_fusion.1 = bf16[2,2048,384]{2,1,0:T(8,128)(2,1)} fusion(bf16[8,2,72,2048]{3,2,1,0:T(8,128)(2,1)} %bitcast.10, bf16[8,2,72,384]{3,2,0,1:T(8,128)(2,1)S(1)} %get-tuple-element.25), kind=kOutput, calls=%fused_computation.9 | convolution fusion | flops 1813512192 | bytes 8749056 | tf_op jit(solution)/shard_map/slcd,slcf->ldf/dot_general | solution.py:81
  297.1 3.3 all-to-all-start.4
  300.4 4.7 %fusion.11 = f32[2,8,72,2048]{3,2,1,0:T(8,128)S(1)} fusion(bf16[8,2,72,384]{3,2,0,1:T(8,128)(2,1)S(1)} %get-tuple-element.24, bf16[2,2048,384]{2,1,0:T(8,128)(2,1)} %all-gather.8.cloned.1.call-done), kind=kOutput, calls=%fused_computation.23 | convolution fusion | flops 1811939328 | bytes 13467648 | tf_op jit(solution)/shard_map/slcf,ldf->slcd/dot_general | solution.py:61
  305.1 3.0 fusion
  308.1 2.6 copy.56
  310.7 5.0 %all-to-all-start.3 = ((bf16[8,144,2048]{2,1,0:T(8,128)(2,1)}), bf16[8,144,2048]{2,1,0:T(8,128)(2,1)}, u32[]{:S(2)}, u32[]{:S(2)}) async-start(bf16[8,144,2048]{2,1,0:T(8,128)(2,1)} %bitcast.108), calls=%async_computation.3 | async-start | bytes 9437184 | tf_op jit(solution)/shard_map/all_to_all | solution.py:65
  316.1 7.2 %bitcast_convert_fusion.2 = bf16[2,2048,384]{2,1,0:T(8,128)(2,1)} fusion(bf16[8,2,72,2048]{3,2,1,0:T(8,128)(2,1)} %bitcast.10, bf16[8,2,72,384]{3,2,0,1:T(8,128)(2,1)S(1)} %get-tuple-element.24), kind=kOutput, calls=%fused_computation.10 | convolution fusion | flops 1813512192 | bytes 8749056 | tf_op jit(solution)/shard_map/slcd,slcf->ldf/dot_general | solution.py:80
  323.4 6.8 %gather_fusion.4 = bf16[1024]{0:T(1024)(128)(2,1)S(1)} fusion(bf16[1152]{0:T(1024)(128)(2,1)S(1)} %reshape.130, s32[1024]{0:T(1024)S(1)} %broadcast_clamp_fusion), kind=kCustom, calls=%fused_computation.4 | custom fusion | bytes 8192 | tf_op jit(solution)/shard_map/gather | solution.py:98
  331.0 90.2 %all-to-all-done.3 = bf16[8,144,2048]{2,1,0:T(8,128)(2,1)} async-done(((bf16[8,144,2048]{2,1,0:T(8,128)(2,1)}), bf16[8,144,2048]{2,1,0:T(8,128)(2,1)}, u32[]{:S(2)}, u32[]{:S(2)}) %all-to-all-start.3) | async-done | bytes 4718624 | tf_op jit(solution)/shard_map/all_to_all | solution.py:65
  421.1 11.9 %gather_fusion.3 = bf16[1024,2048]{1,0:T(8,128)(2,1)} fusion(bf16[1152,2048]{1,0:T(8,128)(2,1)} %bitcast.20, s32[1024]{0:T(1024)S(1)} %broadcast_clamp_fusion), kind=kCustom, calls=%fused_computation.3 | custom fusion | bytes 8392704 | tf_op jit(solution)/shard_map/gather | solution.py:94
  433.0 5.9 %bitcast_reduce_fusion = bf16[128,2048]{1,0:T(8,128)(2,1)} fusion(bf16[1024,2048]{1,0:T(8,128)(2,1)} %gather_fusion.3), kind=kLoop, calls=%fused_computation.18 | loop fusion | flops 1835008 | bytes 4718592 | tf_op jit(solution)/shard_map/reduce_sum | solution.py:95
  (55 shorter events, 5.8 us)
Async XLA Ops:
  7.2 26.6 %copy-start = (bf16[128,2048]{1,0:T(8,128)(2,1)S(1)}, bf16[128,2048]{1,0:T(8,128)(2,1)}, u32[]{:S(2)}) copy-start(bf16[128,2048]{1,0:T(8,128)(2,1)} %param.7) | copy-start | bytes 1572868
  27.4 26.8 %all-to-all-start = ((bf16[8,1,144]{2,1,0:T(2,128)(2,1)}), bf16[8,1,144]{2,1,0:T(2,128)(2,1)S(1)}, u32[]{:S(2)}, u32[]{:S(2)}) async-start(bf16[8,1,144]{2,1,0:T(2,128)(2,1)} %all_to_all.25), calls=%async_computation | async-start | bytes 16384 | tf_op jit(solution)/shard_map/all_to_all | solution.py:37
  33.8 5.9 %copy-start.2 = (bf16[128,2048]{1,0:T(8,128)(2,1)S(1)}, bf16[128,2048]{1,0:T(8,128)(2,1)}, u32[]{:S(2)}) copy-start(bf16[128,2048]{1,0:T(8,128)(2,1)} %param.10) | copy-start | bytes 1572868
  54.1 110.4 %all-to-all-start.2 = ((bf16[8,144,2048]{2,1,0:T(8,128)(2,1)}), bf16[8,144,2048]{2,1,0:T(8,128)(2,1)}, u32[]{:S(2)}, u32[]{:S(2)}) async-start(bf16[8,144,2048]{2,1,0:T(8,128)(2,1)} %get-tuple-element.29), calls=%async_computation.2 | async-start | bytes 9437184 | tf_op jit(solution)/shard_map/all_to_all | solution.py:36
  59.2 111.8 %all-gather.8.cloned.1.call-start = ((), (), s32[]{:S(2)}) async-start(), calls=%async_computation.10 | async-start | bytes 4718592 | tf_op jit(solution)/shard_map/all_gather | solution.py:40
  164.6 109.8 %all-to-all-start.1 = ((bf16[8,144,2048]{2,1,0:T(8,128)(2,1)}), bf16[8,144,2048]{2,1,0:T(8,128)(2,1)}, u32[]{:S(2)}, u32[]{:S(2)}) async-start(bf16[8,144,2048]{2,1,0:T(8,128)(2,1)} %get-tuple-element.28), calls=%async_computation.1 | async-start | bytes 9437184 | tf_op jit(solution)/shard_map/all_to_all | solution.py:52
  169.2 48.7 %all-gather.6.cloned.1.call-start = ((), (), s32[]{:S(2)}) async-start(), calls=%async_computation.9 | async-start | bytes 4718592 | tf_op jit(solution)/shard_map/all_gather | solution.py:41
  169.9 94.5 %all-gather.4.cloned.1.call-start = ((), (), s32[]{:S(2)}) async-start(), calls=%async_computation.8 | async-start | bytes 4718592 | tf_op jit(solution)/shard_map/all_gather | solution.py:42
  170.7 268.2 %reduce-scatter.8.cloned.1.call-start = ((), (), s32[]{:S(2)}) async-start(), calls=%async_computation.13 | async-start | bytes 4718592 | tf_op jit(solution)/shard_map/reduce_scatter | solution.py:90
  288.8 150.0 %reduce-scatter.6.cloned.1.call-start = ((), (), s32[]{:S(2)}) async-start(), calls=%async_computation.12 | async-start | bytes 4718592 | tf_op jit(solution)/shard_map/reduce_scatter | solution.py:87
  297.1 13.6 %all-to-all-start.4 = ((bf16[8,1,144]{2,1,0:T(2,128)(2,1)}), bf16[8,1,144]{2,1,0:T(2,128)(2,1)S(1)}, u32[]{:S(2)}, u32[]{:S(2)}) async-start(bf16[8,1,144]{2,1,0:T(2,128)(2,1)} %convert_element_type.90), calls=%async_computation.4 | async-start | bytes 16384 | tf_op jit(solution)/shard_map/all_to_all | solution.py:72
  300.4 4.7 %copy-start.3 = (bf16[2,2048,384]{2,1,0:T(8,128)(2,1)S(1)}, bf16[2,2048,384]{2,1,0:T(8,128)(2,1)}, u32[]{:S(2)}) copy-start(bf16[2,2048,384]{2,1,0:T(8,128)(2,1)} %all-gather.6.cloned.1.call-done) | copy-start | bytes 9437188
  310.7 110.4 %all-to-all-start.3 = ((bf16[8,144,2048]{2,1,0:T(8,128)(2,1)}), bf16[8,144,2048]{2,1,0:T(8,128)(2,1)}, u32[]{:S(2)}, u32[]{:S(2)}) async-start(bf16[8,144,2048]{2,1,0:T(8,128)(2,1)} %bitcast.108), calls=%async_computation.3 | async-start | bytes 9437184 | tf_op jit(solution)/shard_map/all_to_all | solution.py:65
  315.8 123.1 %reduce-scatter.4.cloned.1.call-start = ((), (), s32[]{:S(2)}) async-start(), calls=%async_computation.11 | async-start | bytes 4718592 | tf_op jit(solution)/shard_map/reduce_scatter | solution.py:84
  421.1 17.8 %copy-start.1 = (bf16[128,2048]{1,0:T(8,128)(2,1)S(1)}, bf16[128,2048]{1,0:T(8,128)(2,1)}, u32[]{:S(2)}) copy-start(bf16[128,2048]{1,0:T(8,128)(2,1)} %param.7) | copy-start | bytes 1572868
Sparse Core Ops, SparseCore 0:
  61.6 46.3 all-gather.7
  171.6 46.2 all-gather.5
  219.4 44.9 all-gather.3
  289.0 42.2 reduce-scatter.7
  334.0 43.3 reduce-scatter.5
  380.0 43.3 reduce-scatter.3
where the time goes:
time: 446 us
  waiting for transfers between devices  286 us (64%)
  matrix products  50.8 us (11%)
  local copies, waits for them, and re-layouts  49.5 us (11%)
  starting transfers between devices  25.3 us (6%)
  other arithmetic  19.9 us (4%)
  between operations  14.3 us (3%)
    all_to_all x1, waiting for transfers between devices, body(): lax.all_to_all(send_rows, 'expert', split_axis=0, concat_axis=0, tiled=True)  105 us
    all_to_all x1, waiting for transfers between devices, body(): lax.all_to_all(d_rows.reshape(n_peers, exp_dev * cap, width), 'expert', s...  90.2 us
    all_gather x1, waiting for transfers between devices, body(): lax.all_gather(up_weight, 'dp', axis=1, tiled=True)  39.7 us
    all_gather x1, waiting for transfers between devices, body(): lax.all_gather(down_weight, 'dp', axis=2, tiled=True)  39.3 us
    gather x1, local copies, waits for them, and re-layouts, body(): per_pair = ret_rows.reshape(experts * cap, width)[slot]  11.9 us
    all_to_all x1, waiting for transfers between devices, body(): lax.all_to_all(send_grad, 'expert', split_axis=0, concat_axis=0, tiled=True)  10 us
  transfers between devices with their start and end apart: 11, of which 5 were waited for; matrix products, arithmetic and copies ran while one was open for 19% of the time, Pallas kernels for 0%

commit v1 on v0

--- a/solution.py
+++ b/solution.py
@@ -3,8 +3,15 @@
 from jax import lax
 from jax.sharding import PartitionSpec as P
 
-
-def body(tokens, expert_ids, gate_weights, cotangent, gate_matrix, up_weight, down_weight):
+F32 = jnp.float32
+BF16 = jnp.bfloat16
+
+
+def mm(a, b, dims):
+    return lax.dot_general(a, b, (dims, ((), ())), preferred_element_type=F32)
+
+
+def dispatch_body(tokens, expert_ids, gate_weights, cotangent, gate_matrix, up_weight, down_weight):
     tok_dev, top = expert_ids.shape
     exp_dev = up_weight.shape[0]
     n_peers = lax.axis_size("expert")
@@ -105,6 +112,71 @@
     )
 
 
+def dense_body(tokens, expert_ids, gate_weights, cotangent, gate_matrix, up_weight, down_weight):
+    tok_dev, top = expert_ids.shape
+    width = tokens.shape[1]
+    exp_dev, _, ff = up_weight.shape
+    n_peers = lax.axis_size("expert")
+    experts = exp_dev * n_peers
+    me = lax.axis_index("expert")
+    rows = tok_dev * n_peers
+
+    chosen = expert_ids[:, :, None] == jnp.arange(experts, dtype=jnp.int32)[None, None, :]
+    dense = jnp.sum(jnp.where(chosen, gate_weights[:, :, None].astype(F32), 0.0), axis=1)
+    dense = dense.astype(BF16)
+
+    x = lax.all_gather(tokens, "expert", axis=0, tiled=True)
+    full_gate = lax.all_gather(gate_matrix, "dp", axis=1, tiled=True)
+    full_up = lax.all_gather(up_weight, "dp", axis=1, tiled=True)
+    c = lax.all_gather(cotangent, "expert", axis=0, tiled=True)
+    full_down = lax.all_gather(down_weight, "dp", axis=2, tiled=True)
+    gates = lax.all_gather(dense, "expert", axis=0, tiled=True)
+    mine = lax.dynamic_slice_in_dim(gates, me * exp_dev, exp_dev, axis=1).astype(F32)
+
+    d_gates, d_ups, weighted, gate_grads = [], [], [], []
+    for e in range(exp_dev):
+        g = mine[:, e : e + 1]
+        pre_gate = mm(x, full_gate[e], ((1,), (0,)))
+        pre_up = mm(x, full_up[e], ((1,), (0,)))
+        sig = jax.nn.sigmoid(pre_gate)
+        active = pre_gate * sig
+        hidden = (active * pre_up).astype(BF16).astype(F32)
+        back = mm(c, full_down[e], ((1,), (1,)))
+        gate_grads.append(jnp.sum(hidden * back, axis=1, keepdims=True))
+        d_hidden = g * back
+        d_gates.append((d_hidden * pre_up * (sig * (1.0 + pre_gate * (1.0 - sig)))).astype(BF16))
+        d_ups.append((d_hidden * active).astype(BF16))
+        weighted.append((g * hidden).astype(BF16))
+
+    def scatter(term, dim):
+        return lax.psum_scatter(term.astype(BF16), "dp", scatter_dimension=dim, tiled=True)
+
+    gate_out = scatter(jnp.stack([mm(x, d, ((0,), (0,))) for d in d_gates]), 1)
+    up_out = scatter(jnp.stack([mm(x, d, ((0,), (0,))) for d in d_ups]), 1)
+    down_out = scatter(jnp.stack([mm(h, c, ((0,), (0,))) for h in weighted]), 2)
+
+    both = sum(mm(d_gates[e], full_gate[e], ((1,), (1,))) for e in range(exp_dev))
+    both = both + sum(mm(d_ups[e], full_up[e], ((1,), (1,))) for e in range(exp_dev))
+    gg = jnp.concatenate(gate_grads, axis=1).astype(BF16)
+    grad_tokens = lax.psum_scatter(both.astype(BF16), "expert", scatter_dimension=0, tiled=True)
+    back_gate = lax.all_to_all(
+        gg.reshape(n_peers, tok_dev, exp_dev), "expert", split_axis=0, concat_axis=0, tiled=True
+    )
+    back_gate = back_gate.transpose(1, 0, 2).reshape(tok_dev, experts)
+    grad_gates = jnp.sum(
+        jnp.where(chosen, back_gate[:, None, :].astype(F32), 0.0), axis=2
+    ).astype(BF16)
+    return grad_tokens, grad_gates, gate_out, up_out, down_out
+
+
+def body(*args):
+    tok_dev, top = args[1].shape
+    experts = args[5].shape[0] * lax.axis_size("expert")
+    cap = min(tok_dev, tok_dev * top * 9 // (8 * experts))
+    dense = tok_dev <= 2 * cap
+    return (dense_body if dense else dispatch_body)(*args)
+
+
 def solution(mesh):
     placed = (
         P(("groups", "expert", "dp"), None),

time: 446 us -> 486 us (1.090)
  waiting for transfers between devices: 286 us -> 366 us
  local copies, waits for them, and re-layouts: 49.5 us -> 6.76 us
  starting transfers between devices: 25.3 us -> 3.89 us
  matrix products: 50.8 us -> 69.1 us
  blocking collectives: 0 us -> 12.9 us
  other arithmetic: 19.9 us -> 12.8 us
    all_to_all x5 -> x1, waiting for transfers between devices: 205 us -> 5.34 us  [dense_body(): lax.all_to_all(gg.reshape(n_peers, tok_dev, exp_dev), 'expert', split_axi...]
    reduce_scatter x3 -> x4, waiting for transfers between devices: 0.01 us -> 139 us  [the longest x3 86.4 us: scatter(): lax.psum_scatter(term.astype(BF16), 'dp', scatter_dimension=dim, tiled=True)]
    all_gather x3 -> x5, waiting for transfers between devices: 79 us -> 218 us  [the longest x1 48.8 us: dense_body(): x = lax.all_gather(tokens, 'expert', axis=0, tiled=True)]
    gather x5 -> x0, local copies, waits for them, and re-layouts: 37.8 us -> none  [the longest x1 11.9 us: body(): per_pair = ret_rows.reshape(experts * cap, width)[slot]]
    all_to_all x5 -> x1, starting transfers between devices: 24.4 us -> 3.31 us  [dense_body(): lax.all_to_all(gg.reshape(n_peers, tok_dev, exp_dev), 'expert', split_axi...]
    dot_general x8 -> x16, matrix products: 50.8 us -> 69.1 us  [mm(): return lax.dot_general(a, b, (dims, ((), ())), preferred_element_type=F32)]
    all_gather x0 -> x1, blocking collectives: none -> 12.9 us  [dense_body(): gates = lax.all_gather(dense, 'expert', axis=0, tiled=True)]
    select_n x3 -> x0, other arithmetic: 8.48 us -> none  [the longest x1 8.46 us: body(): jnp.where(filled[:, None], cotangent[token_row], jnp.zeros((), cotangent....]
  transfers between devices with their start and end apart: 11 -> 10, of which waited for: 5 -> 9; matrix products, arithmetic and copies ran while one was open for 19% -> 13% of each run, Pallas kernels for 0% -> 0%
where the time goes in v1:
time: 486 us
  waiting for transfers between devices  366 us (75%)
  matrix products  69.1 us (14%)
  between operations  14.1 us (3%)
  blocking collectives  12.9 us (3%)
  other arithmetic  12.8 us (3%)
  local copies, waits for them, and re-layouts  6.76 us (1%)
    reduce_scatter x3, waiting for transfers between devices, scatter(): lax.psum_scatter(term.astype(BF16), 'dp', scatter_dimension=dim, tiled=True)  86.4 us
    dot_general x16, matrix products, mm(): return lax.dot_general(a, b, (dims, ((), ())), preferred_element_type=F32)  69.1 us
    reduce_scatter x1, waiting for transfers between devices, dense_body(): lax.psum_scatter(both.astype(BF16), 'expert', scatter_dimension=0, tiled=...  53 us
    all_gather x1, waiting for transfers between devices, dense_body(): x = lax.all_gather(tokens, 'expert', axis=0, tiled=True)  48.8 us
    all_gather x1, waiting for transfers between devices, dense_body(): c = lax.all_gather(cotangent, 'expert', axis=0, tiled=True)  48.6 us
    all_gather x1, waiting for transfers between devices, dense_body(): full_up = lax.all_gather(up_weight, 'dp', axis=1, tiled=True)  46.7 us
    all_gather x1, waiting for transfers between devices, dense_body(): full_down = lax.all_gather(down_weight, 'dp', axis=2, tiled=True)  37.6 us
    all_gather x1, waiting for transfers between devices, dense_body(): full_gate = lax.all_gather(gate_matrix, 'dp', axis=1, tiled=True)  36.4 us
  transfers between devices with their start and end apart: 10, of which 9 were waited for; matrix products, arithmetic and copies ran while one was open for 13% of the time, Pallas kernels for 0%

profile of v1, /device:TPU:0, one launch (start us, length us, event | category | flops | bytes accessed | tf_op | source)
XLA Modules:
  0.0 485.6 jit_solution(5857592679079600042)
XLA Ops:
  10.5 46.7 %all-gather.12.cloned.1.call-done = bf16[2,2048,384]{2,1,0:T(8,128)(2,1)} async-done(((bf16[2,1024,384]{2,1,0:T(8,128)(2,1)}), bf16[2,2048,384]{2,1,0:T(8,128)(2,1)}) %all-gather.12.cloned.1.call-update) | async-done | bytes 3145744 | tf_op jit(solution)/shard_map/all_gather | solution.py:130
  57.2 48.8 %all-gather.10.cloned.1.call-done = bf16[1024,2048]{1,0:T(8,128)(2,1)} async-done(((bf16[128,2048]{1,0:T(8,128)(2,1)}), bf16[1024,2048]{1,0:T(8,128)(2,1)}) %all-gather.10.cloned.1.call-update) | async-done | bytes 4194320 | tf_op jit(solution)/shard_map/all_gather | solution.py:128
  106.0 5.8 %fusion.18 = f32[1024,384]{0,1:T(8,128)} fusion(bf16[1024,2048]{1,0:T(8,128)(2,1)} %all-gather.10.cloned.1.call-done, bf16[2,2048,384]{2,1,0:T(8,128)(2,1)} %all-gather.12.cloned.1.call-done), kind=kOutput, calls=%fused_computation.46 | convolution fusion | flops 1610612736 | bytes 7340032 | tf_op jit(solution)/shard_map/dot_general | solution.py:11
  111.8 3.0 fusion.15
  114.8 36.4 %all-gather.14.cloned.1.call-done = bf16[2,2048,384]{2,1,0:T(8,128)(2,1)} async-done(((bf16[2,1024,384]{2,1,0:T(8,128)(2,1)}), bf16[2,2048,384]{2,1,0:T(8,128)(2,1)}) %all-gather.14.cloned.1.call-update) | async-done | bytes 3145744 | tf_op jit(solution)/shard_map/all_gather | solution.py:129
  151.2 5.8 %fusion.20 = f32[1024,384]{0,1:T(8,128)} fusion(bf16[1024,2048]{1,0:T(8,128)(2,1)} %all-gather.10.cloned.1.call-done, bf16[2,2048,384]{2,1,0:T(8,128)(2,1)} %all-gather.14.cloned.1.call-done), kind=kOutput, calls=%fused_computation.48 | convolution fusion | flops 1610612736 | bytes 7340032 | tf_op jit(solution)/shard_map/dot_general | solution.py:11
  157.0 3.0 fusion.17
  160.0 37.6 %all-gather.8.cloned.1.call-done = bf16[2,384,2048]{2,1,0:T(8,128)(2,1)} async-done(((bf16[2,384,1024]{2,1,0:T(8,128)(2,1)}), bf16[2,384,2048]{2,1,0:T(8,128)(2,1)}) %all-gather.8.cloned.1.call-update) | async-done | bytes 3145744 | tf_op jit(solution)/shard_map/all_gather | solution.py:132
  197.6 48.6 %all-gather.6.cloned.1.call-done = bf16[1024,2048]{1,0:T(8,128)(2,1)} async-done(((bf16[128,2048]{1,0:T(8,128)(2,1)}), bf16[1024,2048]{1,0:T(8,128)(2,1)}) %all-gather.6.cloned.1.call-update) | async-done | bytes 4194320 | tf_op jit(solution)/shard_map/all_gather | solution.py:131
  246.2 7.0 %fusion.6 = (bf16[1024]{0:T(1024)(128)(2,1)S(1)}, bf16[1024,384]{0,1:T(8,128)(2,1)}, f32[1024,384]{0,1:T(8,128)}) fusion(f32[1024,384]{0,1:T(8,128)} %fusion.15, f32[1024,384]{0,1:T(8,128)} %fusion.17, bf16[1024,2048]{1,0:T(8,128)(2,1)} %all-gather.6.cloned.1.call-done, bf16[2,384,2048]{2,1,0:T(8,128)(2,1)} %all-gather.8.cloned.1.call-done), kind=kOutput, calls=%fused_computation.20 | convolution fusion | flops 1614150656 | bytes 11274240 | tf_op jit(solution)/shard_map/dot_general | solution.py:11
  253.3 3.3 fusion.8
  257.2 3.3 all-to-all-start
  260.6 5.3 %all-to-all-done = bf16[8,128,2]{1,2,0:T(2,128)(2,1)S(1)} async-done(((bf16[8,128,2]{1,2,0:T(2,128)(2,1)}), bf16[8,128,2]{1,2,0:T(2,128)(2,1)S(1)}, u32[]{:S(2)}, u32[]{:S(2)}) %all-to-all-start) | async-done | bytes 4128 | tf_op jit(solution)/shard_map/all_to_all | solution.py:162
  266.6 12.9 %all_gather.18 = bf16[1024,16]{0,1:T(8,128)(2,1)S(1)} all-gather(bf16[128,16]{0,1:T(8,128)(2,1)S(1)} %get-tuple-element.26), channel_id=1, replica_groups=mesh['groups'=2,'expert'=8,'dp'=2] {'expert'}, dimensions={0}, use_global_device_ids=true | all-gather | bytes 36864 | tf_op jit(solution)/shard_map/all_gather | solution.py:133
  279.5 4.3 multiply_convert_fusion.2
  283.8 1.9 multiply_convert_fusion.5
  290.2 1.9 pad_maximum_fusion.1
  292.3 4.4 fusion
  296.6 1.8 fusion.1
  298.5 2.0 pad_maximum_fusion
  300.6 4.4 fusion.4
  305.0 1.8 fusion.5
  306.8 2.0 pad_maximum_fusion.2
  309.2 3.6 fusion.19
  312.8 5.7 %fusion.16 = f32[1024,2048]{1,0:T(8,128)} fusion(bf16[1024,384]{0,1:T(8,128)(2,1)S(1)} %copy-done.9, bf16[2,2048,384]{2,1,0:T(8,128)(2,1)S(1)} %copy-done), kind=kOutput, calls=%fused_computation.44 | convolution fusion | flops 1610612736 | bytes 10747904 | tf_op jit(solution)/shard_map/dot_general | solution.py:11
  318.5 5.7 %fusion.14 = f32[1024,2048]{1,0:T(8,128)} fusion(bf16[1024,384]{0,1:T(8,128)(2,1)S(1)} %copy-done.8, bf16[2,2048,384]{2,1,0:T(8,128)(2,1)S(1)} %copy-done.2), kind=kOutput, calls=%fused_computation.42 | convolution fusion | flops 1610612736 | bytes 10747904 | tf_op jit(solution)/shard_map/dot_general | solution.py:11
  324.2 10.4 %add_convert_fusion = bf16[1024,2048]{1,0:T(8,128)(2,1)} fusion(f32[1024,2048]{1,0:T(8,128)} %fusion.14, f32[1024,2048]{1,0:T(8,128)} %fusion.16, f32[1024,2048]{1,0:T(8,128)S(1)} %fusion.19, bf16[1024,384]{0,1:T(8,128)(2,1)S(1)} %copy-done.5, bf16[2,2048,384]{2,1,0:T(8,128)(2,1)S(1)} %copy-done.3), kind=kOutput, calls=%fused_computation | convolution fusion | flops 1619001344 | bytes 31719424 | tf_op jit(solution)/shard_map/dot_general | solution.py:11
  334.6 2.6 copy.30
  337.1 42.7 %reduce-scatter.7.cloned.1.call-done = bf16[2,1024,384]{1,2,0:T(8,128)(2,1)} async-done(((bf16[2,2048,384]{1,2,0:T(8,128)(2,1)}), bf16[2,1024,384]{1,2,0:T(8,128)(2,1)}) %reduce-scatter.7.cloned.1.call-update) | async-done | bytes 1572880 | tf_op jit(solution)/shard_map/reduce_scatter | solution.py:152
  379.9 2.6 copy.29
  382.5 43.6 %reduce-scatter.11.cloned.1.call-done = bf16[2,384,1024]{2,1,0:T(8,128)(2,1)} async-done(((bf16[2,384,2048]{2,1,0:T(8,128)(2,1)}), bf16[2,384,1024]{2,1,0:T(8,128)(2,1)}) %reduce-scatter.11.cloned.1.call-update) | async-done | bytes 1572880 | tf_op jit(solution)/shard_map/reduce_scatter | solution.py:152
  426.1 53.0 %reduce-scatter.5.cloned.1.call-done = bf16[128,2048]{1,0:T(8,128)(2,1)} async-done(((bf16[1024,2048]{1,0:T(8,128)(2,1)}), bf16[128,2048]{1,0:T(8,128)(2,1)}) %reduce-scatter.5.cloned.1.call-update) | async-done | bytes 524304 | tf_op jit(solution)/shard_map/reduce_scatter | solution.py:161
  (78 shorter events, 9.6 us)
Async XLA Ops:
  7.2 50.0 %all-gather.12.cloned.1.call-start = ((), (), s32[]{:S(2)}) async-start(), calls=%async_computation.8 | async-start | bytes 4718592 | tf_op jit(solution)/shard_map/all_gather | solution.py:130
  7.9 98.1 %all-gather.10.cloned.1.call-start = ((), (), s32[]{:S(2)}) async-start(), calls=%async_computation.7 | async-start | bytes 4718592 | tf_op jit(solution)/shard_map/all_gather | solution.py:128
  8.6 142.6 %all-gather.14.cloned.1.call-start = ((), (), s32[]{:S(2)}) async-start(), calls=%async_computation.9 | async-start | bytes 4718592 | tf_op jit(solution)/shard_map/all_gather | solution.py:129
  9.4 188.2 %all-gather.8.cloned.1.call-start = ((), (), s32[]{:S(2)}) async-start(), calls=%async_computation.6 | async-start | bytes 4718592 | tf_op jit(solution)/shard_map/all_gather | solution.py:132
  10.0 236.3 %all-gather.6.cloned.1.call-start = ((), (), s32[]{:S(2)}) async-start(), calls=%async_computation.5 | async-start | bytes 4718592 | tf_op jit(solution)/shard_map/all_gather | solution.py:131
  57.2 54.6 %copy-start.1 = (bf16[2,2048,384]{2,1,0:T(8,128)(2,1)S(1)}, bf16[2,2048,384]{2,1,0:T(8,128)(2,1)}, u32[]{:S(2)}) copy-start(bf16[2,2048,384]{2,1,0:T(8,128)(2,1)} %all-gather.12.cloned.1.call-done) | copy-start | bytes 9437188
  106.0 5.8 %copy-start.17 = (bf16[1024,2048]{1,0:T(8,128)(2,1)S(1)}, bf16[1024,2048]{1,0:T(8,128)(2,1)}, u32[]{:S(2)}) copy-start(bf16[1024,2048]{1,0:T(8,128)(2,1)} %all-gather.10.cloned.1.call-done) | copy-start | bytes 12582916
  151.2 5.8 %copy-start = (bf16[2,2048,384]{2,1,0:T(8,128)(2,1)S(1)}, bf16[2,2048,384]{2,1,0:T(8,128)(2,1)}, u32[]{:S(2)}) copy-start(bf16[2,2048,384]{2,1,0:T(8,128)(2,1)} %all-gather.14.cloned.1.call-done) | copy-start | bytes 9437188
  151.2 5.8 %copy-start.18 = (bf16[1024,2048]{1,0:T(8,128)(2,1)S(1)}, bf16[1024,2048]{1,0:T(8,128)(2,1)}, u32[]{:S(2)}) copy-start(bf16[1024,2048]{1,0:T(8,128)(2,1)} %all-gather.10.cloned.1.call-done) | copy-start | bytes 12582916
  246.2 7.0 %copy-start.12 = (f32[1024,384]{0,1:T(8,128)S(1)}, f32[1024,384]{0,1:T(8,128)}, u32[]{:S(2)}) copy-start(f32[1024,384]{0,1:T(8,128)} %fusion.18) | copy-start | bytes 4718596
  246.2 7.0 %copy-start.13 = (f32[1024,384]{0,1:T(8,128)S(1)}, f32[1024,384]{0,1:T(8,128)}, u32[]{:S(2)}) copy-start(f32[1024,384]{0,1:T(8,128)} %fusion.20) | copy-start | bytes 4718596
  246.2 7.0 %copy-start.21 = (bf16[1024,2048]{1,0:T(8,128)(2,1)S(1)}, bf16[1024,2048]{1,0:T(8,128)(2,1)}, u32[]{:S(2)}) copy-start(bf16[1024,2048]{1,0:T(8,128)(2,1)} %all-gather.6.cloned.1.call-done) | copy-start | bytes 12582916
  246.2 7.0 %copy-start.23 = (bf16[2,384,2048]{2,1,0:T(8,128)(2,1)S(1)}, bf16[2,384,2048]{2,1,0:T(8,128)(2,1)}, u32[]{:S(2)}) copy-start(bf16[2,384,2048]{2,1,0:T(8,128)(2,1)} %all-gather.8.cloned.1.call-done) | copy-start | bytes 9437188
  253.2 7.3 %copy-start.16 = (bf16[128,8]{0,1:T(8,128)(2,1)S(1)}, bf16[128,8]{0,1:T(8,128)(2,1)}, u32[]{:S(2)}) copy-start(bf16[128,8]{0,1:T(8,128)(2,1)} %param.9) | copy-start | bytes 6148
  253.3 12.7 %copy-start.15 = (s32[128,8]{0,1:T(8,128)S(1)}, s32[128,8]{0,1:T(8,128)}, u32[]{:S(2)}) copy-start(s32[128,8]{0,1:T(8,128)} %param.8) | copy-start | bytes 12292
  257.2 8.7 %all-to-all-start = ((bf16[8,128,2]{1,2,0:T(2,128)(2,1)}), bf16[8,128,2]{1,2,0:T(2,128)(2,1)S(1)}, u32[]{:S(2)}, u32[]{:S(2)}) async-start(bf16[8,128,2]{1,2,0:T(2,128)(2,1)} %copy.28), calls=%async_computation.1 | async-start | bytes 8192 | tf_op jit(solution)/shard_map/all_to_all | solution.py:162
  260.5 74.0 %reduce-scatter.9.cloned.1.call-start = ((), (), s32[]{:S(2)}) async-start(), calls=%async_computation.12 | async-start | bytes 4718592 | tf_op jit(solution)/shard_map/reduce_scatter | solution.py:152
  279.4 4.4 copy-start.10
  279.5 4.4 copy-start.11
  279.5 4.4 copy-start.14
  283.8 4.6 copy-start.4
  292.2 87.7 %reduce-scatter.7.cloned.1.call-start = ((), (), s32[]{:S(2)}) async-start(), calls=%async_computation.11 | async-start | bytes 4718592 | tf_op jit(solution)/shard_map/reduce_scatter | solution.py:152
  292.2 4.4 copy-start.6
  292.2 4.4 copy-start.20
  300.5 125.5 %reduce-scatter.11.cloned.1.call-start = ((), (), s32[]{:S(2)}) async-start(), calls=%async_computation.13 | async-start | bytes 4718592 | tf_op jit(solution)/shard_map/reduce_scatter | solution.py:152
  300.6 4.4 copy-start.22
  300.6 4.4 copy-start.24
  308.9 170.2 %reduce-scatter.5.cloned.1.call-start = ((), (), s32[]{:S(2)}) async-start(), calls=%async_computation.10 | async-start | bytes 4718592 | tf_op jit(solution)/shard_map/reduce_scatter | solution.py:161
  312.8 5.7 %copy-start.2 = (bf16[2,2048,384]{2,1,0:T(8,128)(2,1)S(1)}, bf16[2,2048,384]{2,1,0:T(8,128)(2,1)}, u32[]{:S(2)}) copy-start(bf16[2,2048,384]{2,1,0:T(8,128)(2,1)} %all-gather.12.cloned.1.call-done) | copy-start | bytes 9437188
  312.8 5.7 %copy-start.8 = (bf16[1024,384]{0,1:T(8,128)(2,1)S(1)}, bf16[1024,384]{0,1:T(8,128)(2,1)}, u32[]{:S(2)}) copy-start(bf16[1024,384]{0,1:T(8,128)(2,1)} %copy-done.7) | copy-start | bytes 2359300
  318.5 5.7 %copy-start.3 = (bf16[2,2048,384]{2,1,0:T(8,128)(2,1)S(1)}, bf16[2,2048,384]{2,1,0:T(8,128)(2,1)}, u32[]{:S(2)}) copy-start(bf16[2,2048,384]{2,1,0:T(8,128)(2,1)} %all-gather.12.cloned.1.call-done) | copy-start | bytes 9437188
  318.5 5.7 %copy-start.5 = (bf16[1024,384]{0,1:T(8,128)(2,1)S(1)}, bf16[1024,384]{0,1:T(8,128)(2,1)}, u32[]{:S(2)}) copy-start(bf16[1024,384]{0,1:T(8,128)(2,1)} %copy-done.4) | copy-start | bytes 2359300
  (3 other events, 9.1 us)
Sparse Core Ops, SparseCore 0:
  9.5 47.6 all-gather.11
  58.8 47.1 all-gather.9
  107.5 43.6 all-gather.13
  152.6 44.9 all-gather.7
  199.0 47.1 all-gather.5
  292.3 41.8 reduce-scatter.8
  336.5 43.3 reduce-scatter.6
  382.7 43.3 reduce-scatter.10
  429.1 49.9 reduce-scatter.4

commit v2 on v1

--- a/solution.py
+++ b/solution.py
@@ -1,10 +1,224 @@
 import jax
 import jax.numpy as jnp
 from jax import lax
+from jax.experimental import pallas as pl
+from jax.experimental.pallas import tpu as pltpu
 from jax.sharding import PartitionSpec as P
 
 F32 = jnp.float32
 BF16 = jnp.bfloat16
+
+
+MESH = pl.DeviceIdType.MESH
+
+
+def gather_kernel(
+    x_ref, c_ref, g_ref, wg_ref, wu_ref, wd_ref,
+    xo_ref, co_ref, go_ref, fg_ref, fu_ref, fd_ref,
+    line_send, line_recv, pass_send, own_sem, w_send, w_recv, y_send, y_recv,
+):
+    p = lax.axis_index("expert")
+    n = lax.axis_size("expert")
+    steps = n // 2
+    z, core = p // 2, p % 2
+    j = lax.axis_index("dp")
+    grp = lax.axis_index("groups")
+    sib = {"expert": p + 1 - 2 * core}
+    right, left = {"expert": p + 2}, {"expert": p - 2}
+    across, other_group = {"dp": 1 - j}, {"groups": 1 - grp}
+    tok = x_ref.shape[0]
+    depth = wg_ref.shape[1]
+    ff = wg_ref.shape[2]
+
+    barrier = pltpu.get_barrier_semaphore()
+    for device in (sib, across, other_group):
+        pl.semaphore_signal(barrier, inc=1, device_id=device, device_id_type=MESH)
+
+    @pl.when(z > 0)
+    def _():
+        pl.semaphore_signal(barrier, inc=1, device_id=left, device_id_type=MESH)
+
+    @pl.when(z < steps - 1)
+    def _():
+        pl.semaphore_signal(barrier, inc=1, device_id=right, device_id_type=MESH)
+
+    @pl.when((z == 0) | (z == steps - 1))
+    def _():
+        pl.semaphore_wait(barrier, 4)
+
+    @pl.when((z > 0) & (z < steps - 1))
+    def _():
+        pl.semaphore_wait(barrier, 5)
+
+    sources = (x_ref, c_ref, g_ref)
+    lands = (xo_ref, co_ref, go_ref)
+
+    def shard(a, q):
+        return lands[a].at[pl.ds(pl.multiple_of(q * tok, tok), tok)]
+
+    def line_copy(a, q, src, device, way):
+        sems = pass_send.at[a, q] if way == 2 else line_send.at[a, way, q]
+        return pltpu.make_async_remote_copy(
+            src_ref=src, dst_ref=shard(a, q), send_sem=sems, recv_sem=line_recv.at[a, q],
+            device_id=device, device_id_type=MESH,
+        )
+
+    half = ff // 2
+
+    def pieces(src, full, m, part):
+        def at(ref, e, own, jj):
+            if m < 2:
+                rows = depth // 2
+                base = (0 if own else 1) * jj * depth + part * rows
+                return ref.at[e, pl.ds(pl.multiple_of(base, rows), rows)]
+            base = (0 if own else 1) * jj * depth
+            return ref.at[e, pl.ds(part * half, half), pl.ds(pl.multiple_of(base, depth), depth)]
+        return at
+
+    shards_w = ((wg_ref, fg_ref), (wu_ref, fu_ref), (wd_ref, fd_ref))
+
+    def w_copy(m, part):
+        src, full = shards_w[m]
+        at = pieces(src, full, m, part)
+        k = 2 * m + part
+        return pltpu.make_async_remote_copy(
+            src_ref=at(src, grp, True, 0), dst_ref=at(full, grp, False, j),
+            send_sem=w_send.at[k], recv_sem=w_recv.at[k], device_id=across, device_id_type=MESH,
+        )
+
+    def w_arrived(m, part):
+        src, full = shards_w[m]
+        at = pieces(src, full, m, part)
+        k = 2 * m + part
+        return pltpu.make_async_remote_copy(
+            src_ref=at(src, grp, True, 0), dst_ref=at(full, grp, False, 1 - j),
+            send_sem=w_send.at[k], recv_sem=w_recv.at[k], device_id=across, device_id_type=MESH,
+        )
+
+    def y_copy(m, part, e):
+        src, full = shards_w[m]
+        at = pieces(src, full, m, part)
+        k = 2 * m + part
+        return pltpu.make_async_remote_copy(
+            src_ref=at(full, e, False, 1 - j), dst_ref=at(full, e, False, 1 - j),
+            send_sem=y_send.at[k], recv_sem=y_recv.at[k], device_id=other_group,
+            device_id_type=MESH,
+        )
+
+    for a in (2, 0, 1):
+        @pl.when(z < steps - 1)
+        def _(a=a):
+            line_copy(a, p, sources[a], right, 0).start()
+
+        @pl.when(z > 0)
+        def _(a=a):
+            line_copy(a, p, sources[a], left, 1).start()
+
+    for m in range(3):
+        for part in range(2):
+            w_copy(m, part).start()
+    for a in (2, 0, 1):
+        line_copy(a, p, sources[a], sib, 2).start()
+
+    own = [pltpu.make_async_copy(sources[a], shard(a, p), own_sem.at[a]) for a in range(3)]
+    own.append(pltpu.make_async_copy(
+        wg_ref, fg_ref.at[:, pl.ds(pl.multiple_of(j * depth, depth), depth)], own_sem.at[3]))
+    own.append(pltpu.make_async_copy(
+        wu_ref, fu_ref.at[:, pl.ds(pl.multiple_of(j * depth, depth), depth)], own_sem.at[4]))
+    own.append(pltpu.make_async_copy(
+        wd_ref, fd_ref.at[:, :, pl.ds(pl.multiple_of(j * depth, depth), depth)], own_sem.at[5]))
+    for copy in own:
+        copy.start()
+
+    def relay(a, d):
+        @pl.when(z - d >= 0)
+        def _():
+            q = p - 2 * d
+            line_copy(a, q, shard(a, q), right, 0).wait_recv()
+
+            @pl.when(z < steps - 1)
+            def _():
+                line_copy(a, q, shard(a, q), right, 0).start()
+
+            line_copy(a, q, shard(a, q), sib, 2).start()
+
+        @pl.when(z + d < steps)
+        def _():
+            q = p + 2 * d
+            line_copy(a, q, shard(a, q), left, 1).wait_recv()
+
+            @pl.when(z > 0)
+            def _():
+                line_copy(a, q, shard(a, q), left, 1).start()
+
+            line_copy(a, q, shard(a, q), sib, 2).start()
+
+    def carry(k):
+        w_arrived(k // 2, k % 2).wait_recv()
+        y_copy(k // 2, k % 2, grp).start()
+
+    events = []
+    for d in range(1, steps):
+        for a in (2, 0, 1):
+            events.append(("z", a, d))
+    line_events = [e for e in events]
+    weights_at = list(range(6))
+    total = len(line_events)
+    for i, (_, a, d) in enumerate(line_events):
+        if weights_at and i % 3 != 0:
+            carry(weights_at.pop(0))
+        relay(a, d)
+    while weights_at:
+        carry(weights_at.pop(0))
+    for k in range(6):
+        y_copy(k // 2, k % 2, 1 - grp).wait_recv()
+    for a in range(3):
+        for zz in range(steps):
+            q = 2 * zz + 1 - core
+            line_copy(a, q, shard(a, q), sib, 2).wait_recv()
+    for copy in own:
+        copy.wait()
+    for k in range(6):
+        w_copy(k // 2, k % 2).wait_send()
+        y_copy(k // 2, k % 2, grp).wait_send()
+    for a in range(3):
+        for zz in range(steps):
+            q = 2 * zz + core
+            line_copy(a, q, shard(a, q), sib, 2).wait_send()
+
+            @pl.when((zz <= z) & (z < steps - 1))
+            def _(a=a, q=q):
+                line_copy(a, q, shard(a, q), right, 0).wait_send()
+
+            @pl.when((zz >= z) & (z > 0))
+            def _(a=a, q=q):
+                line_copy(a, q, shard(a, q), left, 1).wait_send()
+
+
+def gather_all(tokens, cotangent, dense, gate_matrix, up_weight, down_weight):
+    n = lax.axis_size("expert")
+    exp_dev, depth, ff = gate_matrix.shape
+    rows, width = tokens.shape
+    S = jax.ShapeDtypeStruct
+    return pl.pallas_call(
+        gather_kernel,
+        out_shape=(
+            S((n * rows, width), BF16), S((n * rows, width), BF16),
+            S((n * rows, dense.shape[1]), BF16),
+            S((exp_dev, 2 * depth, ff), BF16), S((exp_dev, 2 * depth, ff), BF16),
+            S((exp_dev, ff, 2 * depth), BF16),
+        ),
+        in_specs=[pl.BlockSpec(memory_space=pl.ANY)] * 6,
+        out_specs=[pl.BlockSpec(memory_space=pl.ANY)] * 6,
+        scratch_shapes=[
+            pltpu.SemaphoreType.DMA((3, 2, n)), pltpu.SemaphoreType.DMA((3, n)),
+            pltpu.SemaphoreType.DMA((3, n)), pltpu.SemaphoreType.DMA((6,)),
+            pltpu.SemaphoreType.DMA((6,)), pltpu.SemaphoreType.DMA((6,)),
+            pltpu.SemaphoreType.DMA((6,)), pltpu.SemaphoreType.DMA((6,)),
+        ],
+        compiler_params=pltpu.CompilerParams(collective_id=0, has_side_effects=True),
+        name="gather_all",
+    )(tokens, cotangent, dense, gate_matrix, up_weight, down_weight)
 
 
 def mm(a, b, dims):
@@ -125,12 +339,11 @@
     dense = jnp.sum(jnp.where(chosen, gate_weights[:, :, None].astype(F32), 0.0), axis=1)
     dense = dense.astype(BF16)
 
-    x = lax.all_gather(tokens, "expert", axis=0, tiled=True)
-    full_gate = lax.all_gather(gate_matrix, "dp", axis=1, tiled=True)
-    full_up = lax.all_gather(up_weight, "dp", axis=1, tiled=True)
-    c = lax.all_gather(cotangent, "expert", axis=0, tiled=True)
-    full_down = lax.all_gather(down_weight, "dp", axis=2, tiled=True)
-    gates = lax.all_gather(dense, "expert", axis=0, tiled=True)
+    lanes = -(-experts // 128) * 128
+    dense = jnp.pad(dense, ((0, 0), (0, lanes - experts)))
+    x, c, gates, full_gate, full_up, full_down = gather_all(
+        tokens, cotangent, dense, gate_matrix, up_weight, down_weight
+    )
     mine = lax.dynamic_slice_in_dim(gates, me * exp_dev, exp_dev, axis=1).astype(F32)
 
     d_gates, d_ups, weighted, gate_grads = [], [], [], []
@@ -148,8 +361,14 @@
         d_ups.append((d_hidden * active).astype(BF16))
         weighted.append((g * hidden).astype(BF16))
 
+    j = lax.axis_index("dp")
+
     def scatter(term, dim):
-        return lax.psum_scatter(term.astype(BF16), "dp", scatter_dimension=dim, tiled=True)
+        half = term.shape[dim] // 2
+        gone = lax.dynamic_slice_in_dim(term, (1 - j) * half, half, axis=dim).astype(BF16)
+        kept = lax.dynamic_slice_in_dim(term, j * half, half, axis=dim).astype(BF16)
+        came = lax.ppermute(gone, "dp", [(0, 1), (1, 0)])
+        return (kept.astype(F32) + came.astype(F32)).astype(BF16)
 
     gate_out = scatter(jnp.stack([mm(x, d, ((0,), (0,))) for d in d_gates]), 1)
     up_out = scatter(jnp.stack([mm(x, d, ((0,), (0,))) for d in d_ups]), 1)
@@ -174,6 +393,8 @@
     experts = args[5].shape[0] * lax.axis_size("expert")
     cap = min(tok_dev, tok_dev * top * 9 // (8 * experts))
     dense = tok_dev <= 2 * cap
+    dense = dense and lax.axis_size("dp") == 2 and lax.axis_size("groups") == 2
+    dense = dense and args[5].shape[0] == 2 and lax.axis_size("expert") >= 4
     return (dense_body if dense else dispatch_body)(*args)
 
 

time: 486 us -> 377 us (0.78)
  waiting for transfers between devices: 366 us -> 74.6 us
  Pallas kernels: 0 us -> 181 us
  blocking collectives: 12.9 us -> 0 us
  matrix products: 69.1 us -> 74.6 us
    all_gather x5 -> x0, waiting for transfers between devices: 218 us -> none  [the longest x1 48.8 us: dense_body(): x = lax.all_gather(tokens, 'expert', axis=0, tiled=True)]
    pallas_call x0 -> x1, Pallas kernels: none -> 181 us  [gather_all(): pl.pallas_call(gather_kernel, out_shape=(S((n * rows, width), BF16), S((n...]
    reduce_scatter x3 -> x0, waiting for transfers between devices: 86.4 us -> none  [scatter(): lax.psum_scatter(term.astype(BF16), 'dp', scatter_dimension=dim, tiled=True)]
    ppermute x0 -> x3, waiting for transfers between devices: none -> 68.8 us  [scatter(): came = lax.ppermute(gone, 'dp', [(0, 1), (1, 0)])]
    reduce_scatter x1, waiting for transfers between devices: 53 us -> 0.01 us  [dense_body(): lax.psum_scatter(both.astype(BF16), 'expert', scatter_dimension=0, tiled=...]
    all_gather x1 -> x0, blocking collectives: 12.9 us -> none  [dense_body(): gates = lax.all_gather(dense, 'expert', axis=0, tiled=True)]
    convert_element_type x2 -> x6, other arithmetic: 6.2 us -> 13.2 us  [the longest x3 9.12 us: scatter(): return (kept.astype(F32) + came.astype(F32)).astype(BF16)]
    another operation x3 -> x0, other arithmetic: 6 us -> none  [the longest x1 2.04 us: dense_body(): down_out = scatter(jnp.stack([mm(h, c, ((0,), (0,))) for h in weighted]), 2)]
  transfers between devices with their start and end apart: 10 -> 5, of which waited for: 9 -> 4; matrix products, arithmetic and copies ran while one was open for 13% -> 11% of each run, Pallas kernels for 0% -> 0%
where the time goes in v2:
time: 377 us; the launch traced here: 373 us
  Pallas kernels  181 us (48%)
  matrix products  74.6 us (20%)
  waiting for transfers between devices  74.6 us (20%)
  other arithmetic  15.4 us (4%)
  between operations  14.5 us (4%)
  starting transfers between devices  8.38 us (2%)
  local copies, waits for them, and re-layouts  4.36 us (1%)
    pallas_call x1, Pallas kernels, gather_all(): pl.pallas_call(gather_kernel, out_shape=(S((n * rows, width), BF16), S((n...  181 us
    dot_general x16, matrix products, mm(): return lax.dot_general(a, b, (dims, ((), ())), preferred_element_type=F32)  74.6 us
    ppermute x3, waiting for transfers between devices, scatter(): came = lax.ppermute(gone, 'dp', [(0, 1), (1, 0)])  68.8 us
    convert_element_type x3, other arithmetic, scatter(): return (kept.astype(F32) + came.astype(F32)).astype(BF16)  9.12 us
  transfers between devices with their start and end apart: 5, of which 4 were waited for; matrix products, arithmetic and copies ran while one was open for 11% of the time, Pallas kernels for 0%

profile of v2, /device:TPU:0, one launch (start us, length us, event | category | flops | bytes accessed | tf_op | source)
XLA Modules:
  0.0 372.8 jit_solution(16865718427026875729)
XLA Ops:
  9.4 181.0 %gather_all.1 = (bf16[1024,2048]{1,0:T(8,128)(2,1)}, bf16[1024,2048]{1,0:T(8,128)(2,1)}, bf16[1024,128]{1,0:T(8,128)(2,1)}, bf16[2,2048,384]{2,1,0:T(8,128)(2,1)...) custom-call(bf16[128,2048]{1,0:T(8,128)(2,1)} %x_ref.1, bf16[128,2048]{1,0:T(8,128)(2,1)} %c_ref.1, ...), custom_call_target="tpu_custom_call" | custom-call | tf_op jit(solution)/shard_map/gather_all/pallas_call | solution.py:203
  190.4 5.8 %fusion.21 = f32[1024,384]{0,1:T(8,128)} fusion(bf16[1024,2048]{1,0:T(8,128)(2,1)} %get-tuple-element.14, bf16[2,2048,384]{2,1,0:T(8,128)(2,1)} %get-tuple-element.15), kind=kOutput, calls=%fused_computation.47 | convolution fusion | flops 1610612736 | bytes 7340032 | tf_op jit(solution)/shard_map/dot_general | solution.py:225
  196.2 3.0 fusion.31
  199.2 3.1 fusion.18
  202.3 3.0 fusion.27
  205.9 0.8 copy-done.30
  206.6 6.6 %fusion.12 = (bf16[1024]{0:T(1024)(128)(2,1)S(1)}, bf16[1024,384]{0,1:T(8,128)(2,1)}, bf16[1024,384]{0,1:T(8,128)(2,1)S(1)}, bf16[1024,384]{0,1:T(8,128)(2,1)S(1)}) fusion(f32[1024,384]{0,1:T(8,128)S(1)} %copy-done.30, f32[1024,384]{0,1:T(8,128)} %fusion.27, f32[1024]{0:T(1024)S(1)} %get-tuple-element.18, bf16[1024,2048]{1,0:T(8,128)(2,1)} %get-tuple-element.12, ...), kind=kOutput, calls=%fused_computation.38 | convolution fusion | flops 1618082816 | bytes 11278336 | tf_op jit(solution)/shard_map/dot_general | solution.py:225
  213.2 2.7 fusion.29
  216.0 5.9 %fusion.25 = f32[1024,2048]{1,0:T(8,128)} fusion(bf16[1024,384]{0,1:T(8,128)(2,1)S(1)} %get-tuple-element.23, bf16[2,2048,384]{2,1,0:T(8,128)(2,1)S(1)} %copy-done.8), kind=kOutput, calls=%fused_computation.51 | convolution fusion | flops 1610612736 | bytes 10747904 | tf_op jit(solution)/shard_map/dot_general | solution.py:225
  221.9 3.3 fusion.14
  225.2 5.6 %fusion.16 = f32[1024,2048]{1,0:T(8,128)} fusion(bf16[1024,384]{0,1:T(8,128)(2,1)S(1)} %get-tuple-element.24, bf16[2,2048,384]{2,1,0:T(8,128)(2,1)S(1)} %copy-done.8), kind=kOutput, calls=%fused_computation.42 | convolution fusion | flops 1610612736 | bytes 10747904 | tf_op jit(solution)/shard_map/dot_general | solution.py:225
  230.8 10.6 %add_convert_fusion = bf16[1024,2048]{1,0:T(8,128)(2,1)} fusion(f32[1024,2048]{1,0:T(8,128)S(1)} %fusion.29, f32[1024,2048]{1,0:T(8,128)} %fusion.25, f32[1024,2048]{1,0:T(8,128)} %fusion.16, bf16[1024,384]{0,1:T(8,128)(2,1)S(1)} %get-tuple-element.25, bf16[2,2048,384]{2,1,0:T(8,128)(2,1)} %get-tuple-element.15), kind=kOutput, calls=%fused_computation | convolution fusion | flops 1619001344 | bytes 31719424 | tf_op jit(solution)/shard_map/dot_general | solution.py:225
  241.5 1.1 copy-done.27
  242.6 4.1 %convolution_bitcast_fusion = bf16[1,384,2048]{2,1,0:T(8,128)(2,1)S(1)} fusion(bf16[1024,2048]{1,0:T(8,128)(2,1)} %get-tuple-element.12, bf16[1024,384]{0,1:T(8,128)(2,1)S(1)} %copy-done.27, f32[1024]{0:T(1024)S(1)} %get-tuple-element.17), kind=kOutput, calls=%fused_computation.28 | convolution fusion | flops 1611792384 | bytes 6557696 | tf_op jit(solution)/shard_map/dot_general | solution.py:225
  246.8 11.1 %convolution_bitcast_fusion.1 = bf16[1,384,2048]{2,1,0:T(8,128)(2,1)S(1)} fusion(bf16[1024,2048]{1,0:T(8,128)(2,1)S(1)} %copy-done.24, bf16[1024,384]{0,1:T(8,128)(2,1)S(1)} %copy-done.26, f32[1024]{0:T(1024)S(1)} %get-tuple-element.18), kind=kOutput, calls=%fused_computation.29 | convolution fusion | flops 1611792384 | bytes 6557696 | tf_op jit(solution)/shard_map/dot_general | solution.py:225
  257.9 1.3 fusion.1
  259.2 1.5 collective-permute-start.2
  260.7 2.5 convolution_bitcast_fusion.4
  263.2 2.5 convolution_bitcast_fusion.5
  265.7 1.3 fusion.9
  267.9 2.5 convolution_bitcast_fusion.2
  270.4 2.5 convolution_bitcast_fusion.3
  272.9 1.5 fusion.5
  274.5 1.5 collective-permute-start.1
  276.6 4.8 %all-to-all-start = ((bf16[8,128,2]{1,2,0:T(2,128)(2,1)}), bf16[8,128,2]{1,2,0:T(2,128)(2,1)S(1)}, u32[]{:S(2)}, u32[]{:S(2)}) async-start(bf16[8,128,2]{1,2,0:T(2,128)(2,1)} %copy.25), calls=%async_computation.1 | async-start | bytes 8192 | tf_op jit(solution)/shard_map/all_to_all | solution.py:381
  281.5 5.8 %all-to-all-done = bf16[8,128,2]{1,2,0:T(2,128)(2,1)S(1)} async-done(((bf16[8,128,2]{1,2,0:T(2,128)(2,1)}), bf16[8,128,2]{1,2,0:T(2,128)(2,1)S(1)}, u32[]{:S(2)}, u32[]{:S(2)}) %all-to-all-start) | async-done | bytes 4128 | tf_op jit(solution)/shard_map/all_to_all | solution.py:381
  287.9 9.0 %collective-permute-done.2 = bf16[2,384,1024]{2,1,0:T(8,128)(2,1)} collective-permute-done((bf16[2,384,1024]{2,1,0:T(8,128)(2,1)}, bf16[2,384,1024]{2,1,0:T(8,128)(2,1)}, u32[]{:S(2)}, u32[]{:S(2)}) %collective-permute-start.2) | collective-permute-done | bytes 1572896 | tf_op jit(solution)/shard_map/ppermute | solution.py:370
  296.9 3.2 add_convert_fusion.1
  300.1 30.5 %collective-permute-done = bf16[2,1024,384]{2,1,0:T(8,128)(2,1)} collective-permute-done((bf16[2,1024,384]{2,1,0:T(8,128)(2,1)}, bf16[2,1024,384]{2,1,0:T(8,128)(2,1)}, u32[]{:S(2)}, u32[]{:S(2)}) %collective-permute-start) | collective-permute-done | bytes 1572896 | tf_op jit(solution)/shard_map/ppermute | solution.py:370
  330.6 2.9 add_convert_fusion.3
  333.5 29.3 %collective-permute-done.1 = bf16[2,1024,384]{2,1,0:T(8,128)(2,1)} collective-permute-done((bf16[2,1024,384]{2,1,0:T(8,128)(2,1)}, bf16[2,1024,384]{2,1,0:T(8,128)(2,1)}, u32[]{:S(2)}, u32[]{:S(2)}) %collective-permute-start.1) | collective-permute-done | bytes 1572896 | tf_op jit(solution)/shard_map/ppermute | solution.py:370
  362.8 2.9 add_convert_fusion.2
  (74 shorter events, 5.2 us)
Async XLA Ops:
  7.2 358.6 %reduce-scatter.2.cloned.1.call-start = ((), (), s32[]{:S(2)}) async-start(), calls=%async_computation.2 | async-start | bytes 4718592 | tf_op jit(solution)/shard_map/reduce_scatter | solution.py:380
  190.4 5.8 %copy-start.9 = (bf16[2,2048,384]{2,1,0:T(8,128)(2,1)S(1)}, bf16[2,2048,384]{2,1,0:T(8,128)(2,1)}, u32[]{:S(2)}) copy-start(bf16[2,2048,384]{2,1,0:T(8,128)(2,1)} %get-tuple-element.15) | copy-start | bytes 9437188
  190.4 5.8 %copy-start.21 = (bf16[1024,2048]{1,0:T(8,128)(2,1)S(1)}, bf16[1024,2048]{1,0:T(8,128)(2,1)}, u32[]{:S(2)}) copy-start(bf16[1024,2048]{1,0:T(8,128)(2,1)} %get-tuple-element.14) | copy-start | bytes 12582916
  196.2 3.0 copy-start.8
  202.3 3.0 copy-start.19
  206.6 6.6 %copy-start.10 = (bf16[2,2048,384]{2,1,0:T(8,128)(2,1)S(1)}, bf16[2,2048,384]{2,1,0:T(8,128)(2,1)}, u32[]{:S(2)}) copy-start(bf16[2,2048,384]{2,1,0:T(8,128)(2,1)} %get-tuple-element.15) | copy-start | bytes 9437188
  213.2 2.7 copy-start.11
  213.2 2.7 copy-start.13
  215.9 5.9 %copy-start.23 = (bf16[1024,2048]{1,0:T(8,128)(2,1)S(1)}, bf16[1024,2048]{1,0:T(8,128)(2,1)}, u32[]{:S(2)}) copy-start(bf16[1024,2048]{1,0:T(8,128)(2,1)} %get-tuple-element.12) | copy-start | bytes 12582916
  215.9 5.9 %copy-start.25 = (bf16[2,384,2048]{2,1,0:T(8,128)(2,1)S(1)}, bf16[2,384,2048]{2,1,0:T(8,128)(2,1)}, u32[]{:S(2)}) copy-start(bf16[2,384,2048]{2,1,0:T(8,128)(2,1)} %get-tuple-element.13) | copy-start | bytes 9437188
  216.0 5.9 %copy-start.28 = (f32[1024,384]{0,1:T(8,128)S(1)}, f32[1024,384]{0,1:T(8,128)}, u32[]{:S(2)}) copy-start(f32[1024,384]{0,1:T(8,128)} %fusion.21) | copy-start | bytes 4718596
  216.0 5.9 %copy-start.29 = (f32[1024,384]{0,1:T(8,128)S(1)}, f32[1024,384]{0,1:T(8,128)}, u32[]{:S(2)}) copy-start(f32[1024,384]{0,1:T(8,128)} %fusion.18) | copy-start | bytes 4718596
  225.2 5.6 %copy-start.17 = (bf16[1024,384]{0,1:T(8,128)(2,1)}, bf16[1024,384]{0,1:T(8,128)(2,1)S(1)}, u32[]{:S(2)}) copy-start(bf16[1024,384]{0,1:T(8,128)(2,1)S(1)} %get-tuple-element.24) | copy-start | bytes 2359300
  225.2 5.6 %copy-start.15 = (bf16[1024,384]{0,1:T(8,128)(2,1)}, bf16[1024,384]{0,1:T(8,128)(2,1)S(1)}, u32[]{:S(2)}) copy-start(bf16[1024,384]{0,1:T(8,128)(2,1)S(1)} %get-tuple-element.25) | copy-start | bytes 2359300
  242.6 4.1 %copy-start.24 = (bf16[1024,2048]{1,0:T(8,128)(2,1)S(1)}, bf16[1024,2048]{1,0:T(8,128)(2,1)}, u32[]{:S(2)}) copy-start(bf16[1024,2048]{1,0:T(8,128)(2,1)} %get-tuple-element.12) | copy-start | bytes 12582916
  242.6 4.1 %copy-start.26 = (bf16[1024,384]{0,1:T(8,128)(2,1)S(1)}, bf16[1024,384]{0,1:T(8,128)(2,1)}, u32[]{:S(2)}) copy-start(bf16[1024,384]{0,1:T(8,128)(2,1)} %get-tuple-element.20) | copy-start | bytes 2359300
  246.8 14.0 %copy-start.22 = (bf16[1024,2048]{1,0:T(8,128)(2,1)S(1)}, bf16[1024,2048]{1,0:T(8,128)(2,1)}, u32[]{:S(2)}) copy-start(bf16[1024,2048]{1,0:T(8,128)(2,1)} %get-tuple-element.14) | copy-start | bytes 12582916
  257.9 2.8 copy-start.18
  259.2 4.0 %copy-start.14 = (bf16[1024,384]{0,1:T(8,128)(2,1)S(1)}, bf16[1024,384]{0,1:T(8,128)(2,1)}, u32[]{:S(2)}) copy-start(bf16[1024,384]{0,1:T(8,128)(2,1)} %copy-done.13) | copy-start | bytes 2359300
  259.2 37.6 %collective-permute-start.2 = (bf16[2,384,1024]{2,1,0:T(8,128)(2,1)}, bf16[2,384,1024]{2,1,0:T(8,128)(2,1)}, u32[]{:S(2)}, u32[]{:S(2)}) collective-permute-start(bf16[2,384,1024]{2,1,0:T(8,128)(2,1)} %fusion.1), channel_id=1, source_target_pairs={{0,1},{1,0},{2,3},{3,2},{4,5},{5,4},{6,7},{7,6},{8,9},{9,8},{10,11... | collective-permute-start | bytes 4718600 | tf_op jit(solution)/shard_map/ppermute | solution.py:370
  263.2 2.5 copy-start
  265.7 2.2 copy-start.16
  267.4 3.0 copy-start.12
  267.4 63.2 %collective-permute-start = (bf16[2,1024,384]{2,1,0:T(8,128)(2,1)}, bf16[2,1024,384]{2,1,0:T(8,128)(2,1)}, u32[]{:S(2)}, u32[]{:S(2)}) collective-permute-start(bf16[2,1024,384]{2,1,0:T(8,128)(2,1)} %fusion.9), channel_id=1, source_target_pairs={{0,1},{1,0},{2,3},{3,2},{4,5},{5,4},{6,7},{7,6},{8,9},{9,8},{10,11... | collective-permute-start | bytes 4718600 | tf_op jit(solution)/shard_map/ppermute | solution.py:370
  270.4 2.5 copy-start.4
  272.9 14.4 %copy-start.20 = (s32[128,8]{0,1:T(8,128)S(1)}, s32[128,8]{0,1:T(8,128)}, u32[]{:S(2)}) copy-start(s32[128,8]{0,1:T(8,128)} %param.8) | copy-start | bytes 12292
  274.5 88.3 %collective-permute-start.1 = (bf16[2,1024,384]{2,1,0:T(8,128)(2,1)}, bf16[2,1024,384]{2,1,0:T(8,128)(2,1)}, u32[]{:S(2)}, u32[]{:S(2)}) collective-permute-start(bf16[2,1024,384]{2,1,0:T(8,128)(2,1)} %fusion.5), channel_id=1, source_target_pairs={{0,1},{1,0},{2,3},{3,2},{4,5},{5,4},{6,7},{7,6},{8,9},{9,8},{10,11... | collective-permute-start | bytes 4718600 | tf_op jit(solution)/shard_map/ppermute | solution.py:370
  276.6 10.6 %all-to-all-start = ((bf16[8,128,2]{1,2,0:T(2,128)(2,1)}), bf16[8,128,2]{1,2,0:T(2,128)(2,1)S(1)}, u32[]{:S(2)}, u32[]{:S(2)}) async-start(bf16[8,128,2]{1,2,0:T(2,128)(2,1)} %copy.25), calls=%async_computation.1 | async-start | bytes 8192 | tf_op jit(solution)/shard_map/all_to_all | solution.py:381
  287.8 42.7 %copy-start.1 = (bf16[1,2048,384]{2,1,0:T(8,128)(2,1)S(1)}, bf16[1,2048,384]{2,1,0:T(8,128)(2,1)}, u32[]{:S(2)}) copy-start(bf16[1,2048,384]{2,1,0:T(8,128)(2,1)} %copy-done) | copy-start | bytes 4718596
  287.8 42.7 %copy-start.3 = (bf16[1,2048,384]{2,1,0:T(8,128)(2,1)S(1)}, bf16[1,2048,384]{2,1,0:T(8,128)(2,1)}, u32[]{:S(2)}) copy-start(bf16[1,2048,384]{2,1,0:T(8,128)(2,1)} %copy-done.2) | copy-start | bytes 4718596
  300.1 62.7 %copy-start.5 = (bf16[1,2048,384]{2,1,0:T(8,128)(2,1)S(1)}, bf16[1,2048,384]{2,1,0:T(8,128)(2,1)}, u32[]{:S(2)}) copy-start(bf16[1,2048,384]{2,1,0:T(8,128)(2,1)} %copy-done.4) | copy-start | bytes 4718596
  300.1 62.7 %copy-start.7 = (bf16[1,2048,384]{2,1,0:T(8,128)(2,1)S(1)}, bf16[1,2048,384]{2,1,0:T(8,128)(2,1)}, u32[]{:S(2)}) copy-start(bf16[1,2048,384]{2,1,0:T(8,128)(2,1)} %copy-done.6) | copy-start | bytes 4718596
  (4 other events, 5.9 us)
Sparse Core Ops, SparseCore 0:
  241.6 50.3 reduce-scatter.1

commit v3 on v2

--- a/solution.py
+++ b/solution.py
@@ -15,7 +15,8 @@
 def gather_kernel(
     x_ref, c_ref, g_ref, wg_ref, wu_ref, wd_ref,
     xo_ref, co_ref, go_ref, fg_ref, fu_ref, fd_ref,
-    line_send, line_recv, pass_send, own_sem, w_send, w_recv, y_send, y_recv,
+    line_send, line_recv, pass_send, own_sem, w_send, w_recv, y_send, y_recv, in_sem,
+    x_st, c_st, g_st, wg_st, wu_st, wd_st,
 ):
     p = lax.axis_index("expert")
     n = lax.axis_size("expert")
@@ -120,15 +121,20 @@
     for a in (2, 0, 1):
         line_copy(a, p, sources[a], sib, 2).start()
 
-    own = [pltpu.make_async_copy(sources[a], shard(a, p), own_sem.at[a]) for a in range(3)]
-    own.append(pltpu.make_async_copy(
-        wg_ref, fg_ref.at[:, pl.ds(pl.multiple_of(j * depth, depth), depth)], own_sem.at[3]))
-    own.append(pltpu.make_async_copy(
-        wu_ref, fu_ref.at[:, pl.ds(pl.multiple_of(j * depth, depth), depth)], own_sem.at[4]))
-    own.append(pltpu.make_async_copy(
-        wd_ref, fd_ref.at[:, :, pl.ds(pl.multiple_of(j * depth, depth), depth)], own_sem.at[5]))
-    for copy in own:
+    here = pl.ds(pl.multiple_of(j * depth, depth), depth)
+    stages = (x_st, c_st, g_st, wg_st, wu_st, wd_st)
+    homes = (
+        shard(0, p), shard(1, p), shard(2, p),
+        fg_ref.at[:, here], fu_ref.at[:, here], fd_ref.at[:, :, here],
+    )
+    blocks = (x_ref, c_ref, g_ref, wg_ref, wu_ref, wd_ref)
+    into = [pltpu.make_async_copy(blocks[i], stages[i], in_sem.at[i]) for i in range(6)]
+    own = [pltpu.make_async_copy(stages[i], homes[i], own_sem.at[i]) for i in range(6)]
+    for copy in into:
         copy.start()
+    for i in range(6):
+        into[i].wait()
+        own[i].start()
 
     def relay(a, d):
         @pl.when(z - d >= 0)
@@ -215,8 +221,15 @@
             pltpu.SemaphoreType.DMA((3, n)), pltpu.SemaphoreType.DMA((6,)),
             pltpu.SemaphoreType.DMA((6,)), pltpu.SemaphoreType.DMA((6,)),
             pltpu.SemaphoreType.DMA((6,)), pltpu.SemaphoreType.DMA((6,)),
+            pltpu.SemaphoreType.DMA((6,)),
+        ]
+        + [
+            pltpu.VMEM(v.shape, v.dtype)
+            for v in (tokens, cotangent, dense, gate_matrix, up_weight, down_weight)
         ],
-        compiler_params=pltpu.CompilerParams(collective_id=0, has_side_effects=True),
+        compiler_params=pltpu.CompilerParams(
+            collective_id=0, has_side_effects=True, vmem_limit_bytes=56 * 1024 * 1024
+        ),
         name="gather_all",
     )(tokens, cotangent, dense, gate_matrix, up_weight, down_weight)
 
@@ -346,38 +359,62 @@
     )
     mine = lax.dynamic_slice_in_dim(gates, me * exp_dev, exp_dev, axis=1).astype(F32)
 
-    d_gates, d_ups, weighted, gate_grads = [], [], [], []
-    for e in range(exp_dev):
-        g = mine[:, e : e + 1]
-        pre_gate = mm(x, full_gate[e], ((1,), (0,)))
-        pre_up = mm(x, full_up[e], ((1,), (0,)))
-        sig = jax.nn.sigmoid(pre_gate)
-        active = pre_gate * sig
-        hidden = (active * pre_up).astype(BF16).astype(F32)
-        back = mm(c, full_down[e], ((1,), (1,)))
-        gate_grads.append(jnp.sum(hidden * back, axis=1, keepdims=True))
-        d_hidden = g * back
-        d_gates.append((d_hidden * pre_up * (sig * (1.0 + pre_gate * (1.0 - sig)))).astype(BF16))
+    j = lax.axis_index("dp")
+    depth = gate_matrix.shape[1]
+    swap = [(0, 1), (1, 0)]
+
+    def sides(v):
+        return (
+            lax.dynamic_slice_in_dim(v, (1 - j) * depth, depth, axis=1),
+            lax.dynamic_slice_in_dim(v, j * depth, depth, axis=1),
+        )
+
+    x_gone, x_kept = sides(x)
+    local = range(exp_dev)
+    pre_gates = [mm(x, full_gate[e], ((1,), (0,))) for e in local]
+    pre_ups = [mm(x, full_up[e], ((1,), (0,))) for e in local]
+    sigs = [jax.nn.sigmoid(v) for v in pre_gates]
+    actives = [v * s for v, s in zip(pre_gates, sigs)]
+    hiddens = [(v * u).astype(BF16) for v, u in zip(actives, pre_ups)]
+    weighted = [(mine[:, e : e + 1] * hiddens[e].astype(F32)).astype(BF16) for e in local]
+
+    c_gone, c_kept = sides(c)
+    down_gone = [mm(h, c_gone, ((0,), (0,))).astype(BF16) for h in weighted]
+    down_came = [lax.ppermute(v, "dp", swap) for v in down_gone]
+    c_back, _ = lax.optimization_barrier((c, down_gone))
+
+    d_gates, d_ups, gate_grads = [], [], []
+    for e in local:
+        sig, active = sigs[e], actives[e]
+        back = mm(c_back, full_down[e], ((1,), (1,)))
+        gate_grads.append(jnp.sum(hiddens[e].astype(F32) * back, axis=1, keepdims=True))
+        d_hidden = mine[:, e : e + 1] * back
+        slope = sig * (1.0 + pre_gates[e] * (1.0 - sig))
+        d_gates.append((d_hidden * pre_ups[e] * slope).astype(BF16))
         d_ups.append((d_hidden * active).astype(BF16))
-        weighted.append((g * hidden).astype(BF16))
-
-    j = lax.axis_index("dp")
-
-    def scatter(term, dim):
-        half = term.shape[dim] // 2
-        gone = lax.dynamic_slice_in_dim(term, (1 - j) * half, half, axis=dim).astype(BF16)
-        kept = lax.dynamic_slice_in_dim(term, j * half, half, axis=dim).astype(BF16)
-        came = lax.ppermute(gone, "dp", [(0, 1), (1, 0)])
-        return (kept.astype(F32) + came.astype(F32)).astype(BF16)
-
-    gate_out = scatter(jnp.stack([mm(x, d, ((0,), (0,))) for d in d_gates]), 1)
-    up_out = scatter(jnp.stack([mm(x, d, ((0,), (0,))) for d in d_ups]), 1)
-    down_out = scatter(jnp.stack([mm(h, c, ((0,), (0,))) for h in weighted]), 2)
-
-    both = sum(mm(d_gates[e], full_gate[e], ((1,), (1,))) for e in range(exp_dev))
-    both = both + sum(mm(d_ups[e], full_up[e], ((1,), (1,))) for e in range(exp_dev))
+
+    gate_gone = [mm(x_gone, d, ((0,), (0,))).astype(BF16) for d in d_gates]
+    gate_came = [lax.ppermute(v, "dp", swap) for v in gate_gone]
+    up_gone = [mm(x_gone, d, ((0,), (0,))).astype(BF16) for d in d_ups]
+    up_came = [lax.ppermute(v, "dp", swap) for v in up_gone]
+    d_gates_r, d_ups_r, _, first_came = lax.optimization_barrier(
+        (d_gates, d_ups, (gate_gone, up_gone), down_came[0])
+    )
+    down_came[0] = first_came
+
+    both = sum(mm(d_gates_r[e], full_gate[e], ((1,), (1,))) for e in local)
+    both = (both + sum(mm(d_ups_r[e], full_up[e], ((1,), (1,))) for e in local)).astype(BF16)
+    d_gates_k, d_ups_k, weighted_k, _ = lax.optimization_barrier((d_gates, d_ups, weighted, both))
+
+    def settle(first, second, came):
+        parts = [mm(a, b, ((0,), (0,))).astype(BF16).astype(F32) for a, b in zip(first, second)]
+        return jnp.stack([(v + w.astype(F32)).astype(BF16) for v, w in zip(parts, came)])
+
+    down_out = settle(weighted_k, [c_kept] * exp_dev, down_came)
+    gate_out = settle([x_kept] * exp_dev, d_gates_k, gate_came)
+    up_out = settle([x_kept] * exp_dev, d_ups_k, up_came)
     gg = jnp.concatenate(gate_grads, axis=1).astype(BF16)
-    grad_tokens = lax.psum_scatter(both.astype(BF16), "expert", scatter_dimension=0, tiled=True)
+    grad_tokens = lax.psum_scatter(both, "expert", scatter_dimension=0, tiled=True)
     back_gate = lax.all_to_all(
         gg.reshape(n_peers, tok_dev, exp_dev), "expert", split_axis=0, concat_axis=0, tiled=True
     )

time: 377 us -> 256 us (0.68)
  Pallas kernels: 181 us -> 77.9 us
  waiting for transfers between devices: 74.6 us -> 63 us
  other arithmetic: 15.4 us -> 7.31 us
    pallas_call x1, Pallas kernels: 181 us -> 77.9 us  [gather_all(): pl.pallas_call(gather_kernel, out_shape=(S((n * rows, width), BF16), S((n...]
    convert_element_type x6 -> x0, other arithmetic: 13.2 us -> none  [the longest x3 9.12 us: scatter(): return (kept.astype(F32) + came.astype(F32)).astype(BF16)]
    ppermute x3 -> x6, waiting for transfers between devices: 68.8 us -> 60.3 us  [the longest x2 42.4 us: dense_body(): up_came = [lax.ppermute(v, 'dp', swap) for v in up_gone]]
    another operation x0 -> x4, other arithmetic: none -> 4.22 us  [settle(): jnp.stack([(v + w.astype(F32)).astype(BF16) for v, w in zip(parts, came)])]
    dot_general x16 -> x22, matrix products: 74.6 us -> 74.8 us  [mm(): return lax.dot_general(a, b, (dims, ((), ())), preferred_element_type=F32)]
  transfers between devices with their start and end apart: 5 -> 8, of which waited for: 4 -> 5; matrix products, arithmetic and copies ran while one was open for 11% -> 16% of each run, Pallas kernels for 0% -> 0%
where the time goes in v3:
time: 256 us; the launch traced here: 251 us
  Pallas kernels  77.9 us (30%)
  matrix products  74.8 us (29%)
  waiting for transfers between devices  63 us (25%)
  between operations  14.5 us (6%)
  starting transfers between devices  10.3 us (4%)
  other arithmetic  7.31 us (3%)
  local copies, waits for them, and re-layouts  3.54 us (1%)
    pallas_call x1, Pallas kernels, gather_all(): pl.pallas_call(gather_kernel, out_shape=(S((n * rows, width), BF16), S((n...  77.9 us
    dot_general x22, matrix products, mm(): return lax.dot_general(a, b, (dims, ((), ())), preferred_element_type=F32)  74.8 us
    ppermute x2, waiting for transfers between devices, dense_body(): up_came = [lax.ppermute(v, 'dp', swap) for v in up_gone]  42.4 us
    ppermute x2, waiting for transfers between devices, dense_body(): gate_came = [lax.ppermute(v, 'dp', swap) for v in gate_gone]  9.75 us
    ppermute x2, waiting for transfers between devices, dense_body(): down_came = [lax.ppermute(v, 'dp', swap) for v in down_gone]  8.17 us
  transfers between devices with their start and end apart: 8, of which 5 were waited for; matrix products, arithmetic and copies ran while one was open for 16% of the time, Pallas kernels for 0%

profile of v3, /device:TPU:0, one launch (start us, length us, event | category | flops | bytes accessed | tf_op | source)
XLA Modules:
  0.0 251.4 jit_solution(14341860339238668003)
XLA Ops:
  9.4 77.9 %gather_all.1 = (bf16[1024,2048]{1,0:T(8,128)(2,1)}, bf16[1024,2048]{1,0:T(8,128)(2,1)}, bf16[1024,128]{1,0:T(8,128)(2,1)}, bf16[2,2048,384]{2,1,0:T(8,128)(2,1)...) custom-call(bf16[128,2048]{1,0:T(8,128)(2,1)} %x_ref.1, bf16[128,2048]{1,0:T(8,128)(2,1)} %c_ref.1, ...), custom_call_target="tpu_custom_call" | custom-call | tf_op jit(solution)/shard_map/gather_all/pallas_call | solution.py:209
  88.9 4.6 %fusion.29 = f32[1024,384]{0,1:T(8,128)S(1)} fusion(bf16[1024,2048]{1,0:T(8,128)(2,1)} %get-tuple-element.25, bf16[2,2048,384]{2,1,0:T(8,128)(2,1)} %get-tuple-element.26), kind=kOutput, calls=%fused_computation.37 | convolution fusion | flops 1610612736 | bytes 7340032 | tf_op jit(solution)/shard_map/dot_general | solution.py:238
  93.8 2.1 fusion.8
  97.8 1.6 collective-permute-start
  99.4 1.9 fusion.22
  101.3 2.1 fusion.10
  103.4 1.9 fusion.38
  105.8 2.8 %multiply_convert_fusion = (bf16[1024,384]{0,1:T(8,128)(2,1)S(1)}, bf16[1024,384]{0,1:T(8,128)(2,1)S(1)}, bf16[1024]{0:T(1024)(128)(2,1)S(1)}) fusion(f32[1024]{0:T(1024)S(1)} %get-tuple-element.41, f32[1024,384]{0,1:T(8,128)S(1)} %fusion.22, f32[1024,384]{0,1:T(8,128)S(1)} %get-tuple-element.54, bf16[1024,384]{0,1:T(8,128)(2,1)S(1)} %get-tuple-element.44, ...), kind=kOutput, calls=%fused_computation.45 | convolution fusion | flops 1617296384 | bytes 11278336 | tf_op jit(solution)/shard_map/dot_general | solution.py:238
  108.6 2.2 convolution_convert_fusion.4
  110.9 2.5 multiply_convert_fusion.1
  113.4 2.2 convolution_convert_fusion.6
  115.5 2.2 convolution_convert_fusion.5
  117.8 2.2 convolution_convert_fusion.7
  119.9 2.4 fusion.27
  122.4 14.7 %fusion.20 = f32[1024,2048]{1,0:T(8,128)} fusion(bf16[1024,384]{0,1:T(8,128)(2,1)S(1)} %get-tuple-element.35, bf16[2,2048,384]{2,1,0:T(8,128)(2,1)S(1)} %copy-done), kind=kOutput, calls=%fused_computation.28 | convolution fusion | flops 1610612736 | bytes 10747904 | tf_op jit(solution)/shard_map/dot_general | solution.py:238
  137.1 5.6 %fusion.16 = f32[1024,2048]{1,0:T(8,128)} fusion(bf16[1024,384]{0,1:T(8,128)(2,1)S(1)} %get-tuple-element.37, bf16[2,2048,384]{2,1,0:T(8,128)(2,1)S(1)} %copy-done.1), kind=kOutput, calls=%fused_computation.24 | convolution fusion | flops 1610612736 | bytes 10747904 | tf_op jit(solution)/shard_map/dot_general | solution.py:238
  142.7 10.4 %add_convert_fusion = bf16[1024,2048]{1,0:T(8,128)(2,1)} fusion(f32[1024,2048]{1,0:T(8,128)} %fusion.16, f32[1024,2048]{1,0:T(8,128)S(1)} %fusion.27, f32[1024,2048]{1,0:T(8,128)} %fusion.20, bf16[1024,384]{0,1:T(8,128)(2,1)} %copy-done.6, bf16[2,2048,384]{2,1,0:T(8,128)(2,1)S(1)} %copy-done.1), kind=kOutput, calls=%fused_computation | convolution fusion | flops 1619001344 | bytes 31719424 | tf_op jit(solution)/shard_map/dot_general | solution.py:238
  155.9 3.7 %all-to-all-start = ((bf16[8,128,2]{1,2,0:T(2,128)(2,1)}), bf16[8,128,2]{1,2,0:T(2,128)(2,1)S(1)}, u32[]{:S(2)}, u32[]{:S(2)}) async-start(bf16[8,128,2]{1,2,0:T(2,128)(2,1)} %copy.25), calls=%async_computation.1 | async-start | bytes 8192 | tf_op jit(solution)/shard_map/all_to_all | solution.py:418
  160.5 1.2 collective-permute-start.3
  162.5 2.7 %all-to-all-done = bf16[8,128,2]{1,2,0:T(2,128)(2,1)S(1)} async-done(((bf16[8,128,2]{1,2,0:T(2,128)(2,1)}), bf16[8,128,2]{1,2,0:T(2,128)(2,1)S(1)}, u32[]{:S(2)}, u32[]{:S(2)}) %all-to-all-start) | async-done | bytes 4128 | tf_op jit(solution)/shard_map/all_to_all | solution.py:418
  165.8 8.2 %collective-permute-done.5 = bf16[384,1024]{1,0:T(8,128)(2,1)} collective-permute-done((bf16[384,1024]{1,0:T(8,128)(2,1)}, bf16[384,1024]{1,0:T(8,128)(2,1)}, u32[]{:S(2)}, u32[]{:S(2)}) %collective-permute-start.5) | collective-permute-done | bytes 786464 | tf_op jit(solution)/shard_map/ppermute | solution.py:383
  173.9 3.0 %fusion.85 = bf16[1,384,1024]{2,1,0:T(8,128)(2,1)S(1)} fusion(bf16[384,1024]{1,0:T(8,128)(2,1)} %collective-permute-done.5, bf16[1024,384]{0,1:T(8,128)(2,1)} %copy-done.18, bf16[1024,2048]{1,0:T(8,128)(2,1)} %get-tuple-element.28, s32[]{:T(128)S(6)} %select_n.23), kind=kOutput, calls=%fused_computation.89 | convolution fusion | flops 807272448 | bytes 4456452 | tf_op jit(solution)/shard_map/dot_general | solution.py:238
  178.0 12.8 %collective-permute-done.4 = bf16[1024,384]{1,0:T(8,128)(2,1)} collective-permute-done((bf16[1024,384]{1,0:T(8,128)(2,1)}, bf16[1024,384]{1,0:T(8,128)(2,1)}, u32[]{:S(2)}, u32[]{:S(2)}) %collective-permute-start.4) | collective-permute-done | bytes 786464 | tf_op jit(solution)/shard_map/ppermute | solution.py:399
  190.8 2.5 fusion.80
  193.6 1.3 pad_maximum_fusion.2
  194.8 29.6 %collective-permute-done.3 = bf16[1024,384]{1,0:T(8,128)(2,1)} collective-permute-done((bf16[1024,384]{1,0:T(8,128)(2,1)}, bf16[1024,384]{1,0:T(8,128)(2,1)}, u32[]{:S(2)}, u32[]{:S(2)}) %collective-permute-start.3) | collective-permute-done | bytes 786464 | tf_op jit(solution)/shard_map/ppermute | solution.py:399
  224.5 2.5 fusion.75
  227.0 1.3 pad_maximum_fusion.1
  228.3 2.5 %fusion.65 = bf16[1,1024,384]{2,1,0:T(8,128)(2,1)S(1)} fusion(bf16[1024,384]{1,0:T(8,128)(2,1)} %collective-permute-done.1, bf16[1024,384]{0,1:T(8,128)(2,1)S(1)} %copy-done.5, bf16[1024,2048]{1,0:T(8,128)(2,1)S(1)} %copy-done.12, s32[]{:T(128)S(6)} %select_n.23), kind=kOutput, calls=%fused_computation.85 | convolution fusion | flops 807272448 | bytes 4456452 | tf_op jit(solution)/shard_map/dot_general | solution.py:238
  230.8 9.8 %collective-permute-done.2 = bf16[1024,384]{1,0:T(8,128)(2,1)} collective-permute-done((bf16[1024,384]{1,0:T(8,128)(2,1)S(1)}, bf16[1024,384]{1,0:T(8,128)(2,1)}, u32[]{:S(2)}, u32[]{:S(2)}) %collective-permute-start.2) | collective-permute-done | bytes 786464 | tf_op jit(solution)/shard_map/ppermute | solution.py:397
  240.6 2.5 fusion.70
  243.0 1.3 pad_maximum_fusion
  (64 shorter events, 12.8 us)
Async XLA Ops:
  7.2 237.2 %reduce-scatter.2.cloned.1.call-start = ((), (), s32[]{:S(2)}) async-start(), calls=%async_computation.2 | async-start | bytes 4718592 | tf_op jit(solution)/shard_map/reduce_scatter | solution.py:417
  88.9 4.7 %copy-start.1 = (bf16[2,2048,384]{2,1,0:T(8,128)(2,1)S(1)}, bf16[2,2048,384]{2,1,0:T(8,128)(2,1)}, u32[]{:S(2)}) copy-start(bf16[2,2048,384]{2,1,0:T(8,128)(2,1)} %get-tuple-element.27) | copy-start | bytes 9437188
  88.9 4.9 %copy-start.11 = (bf16[1024,2048]{1,0:T(8,128)(2,1)S(1)}, bf16[1024,2048]{1,0:T(8,128)(2,1)}, u32[]{:S(2)}) copy-start(bf16[1024,2048]{1,0:T(8,128)(2,1)} %get-tuple-element.25) | copy-start | bytes 12582916
  93.8 3.0 %copy-start.13 = (bf16[1024,2048]{1,0:T(8,128)(2,1)S(1)}, bf16[1024,2048]{1,0:T(8,128)(2,1)}, u32[]{:S(2)}) copy-start(bf16[1024,2048]{1,0:T(8,128)(2,1)} %get-tuple-element.28) | copy-start | bytes 12582916
  95.9 0.9 copy-start.19
  96.8 2.6 %copy-start = (bf16[2,2048,384]{2,1,0:T(8,128)(2,1)S(1)}, bf16[2,2048,384]{2,1,0:T(8,128)(2,1)}, u32[]{:S(2)}) copy-start(bf16[2,2048,384]{2,1,0:T(8,128)(2,1)} %get-tuple-element.26) | copy-start | bytes 9437188
  97.8 22.1 %collective-permute-start = (bf16[384,1024]{1,0:T(8,128)(2,1)S(1)}, bf16[384,1024]{1,0:T(8,128)(2,1)S(1)}, u32[]{:S(2)}, u32[]{:S(2)}) collective-permute-start(bf16[384,1024]{1,0:T(8,128)(2,1)S(1)} %fusion.35), channel_id=1, source_target_pairs={{0,1},{1,0},{2,3},{3,2},{4,5},{5,4},{6,7},{7,6},{8,9},{9,8},{10,11... | collective-permute-start | bytes 2359304 | tf_op jit(solution)/shard_map/ppermute | solution.py:383
  103.4 1.9 copy-start.18
  103.4 2.5 copy-start.15
  108.6 13.8 %copy-start.2 = (bf16[1024,384]{0,1:T(8,128)(2,1)}, bf16[1024,384]{0,1:T(8,128)(2,1)S(1)}, u32[]{:S(2)}) copy-start(bf16[1024,384]{0,1:T(8,128)(2,1)S(1)} %get-tuple-element.35) | copy-start | bytes 2359300
  108.6 28.5 %copy-start.8 = (bf16[1024,384]{0,1:T(8,128)(2,1)}, bf16[1024,384]{0,1:T(8,128)(2,1)S(1)}, u32[]{:S(2)}) copy-start(bf16[1024,384]{0,1:T(8,128)(2,1)S(1)} %get-tuple-element.37) | copy-start | bytes 2359300
  113.3 4.4 %copy-start.6 = (bf16[1024,384]{0,1:T(8,128)(2,1)}, bf16[1024,384]{0,1:T(8,128)(2,1)S(1)}, u32[]{:S(2)}) copy-start(bf16[1024,384]{0,1:T(8,128)(2,1)S(1)} %get-tuple-element.36) | copy-start | bytes 2359300
  113.3 6.6 %copy-start.4 = (bf16[1024,384]{0,1:T(8,128)(2,1)}, bf16[1024,384]{0,1:T(8,128)(2,1)S(1)}, u32[]{:S(2)}) copy-start(bf16[1024,384]{0,1:T(8,128)(2,1)S(1)} %get-tuple-element.34) | copy-start | bytes 2359300
  153.1 6.4 %copy-start.17 = (bf16[1024,384]{1,0:T(8,128)(2,1)S(1)}, bf16[1024,384]{1,0:T(8,128)(2,1)}, u32[]{:S(2)}) copy-start(bf16[1024,384]{1,0:T(8,128)(2,1)} %convolution_convert_fusion.7) | copy-start | bytes 2359300
  153.1 8.5 %copy-start.16 = (bf16[1024,384]{1,0:T(8,128)(2,1)S(1)}, bf16[1024,384]{1,0:T(8,128)(2,1)}, u32[]{:S(2)}) copy-start(bf16[1024,384]{1,0:T(8,128)(2,1)} %convolution_convert_fusion.6) | copy-start | bytes 2359300
  153.1 12.0 %copy-start.10 = (s32[128,8]{0,1:T(8,128)S(1)}, s32[128,8]{0,1:T(8,128)}, u32[]{:S(2)}) copy-start(s32[128,8]{0,1:T(8,128)} %param.8) | copy-start | bytes 12292
  153.2 20.8 %collective-permute-start.5 = (bf16[384,1024]{1,0:T(8,128)(2,1)}, bf16[384,1024]{1,0:T(8,128)(2,1)}, u32[]{:S(2)}, u32[]{:S(2)}) collective-permute-start(bf16[384,1024]{1,0:T(8,128)(2,1)} %fusion.38), channel_id=1, source_target_pairs={{0,1},{1,0},{2,3},{3,2},{4,5},{5,4},{6,7},{7,6},{8,9},{9,8},{10,11... | collective-permute-start | bytes 2359304 | tf_op jit(solution)/shard_map/ppermute | solution.py:383
  154.0 36.7 %collective-permute-start.4 = (bf16[1024,384]{1,0:T(8,128)(2,1)}, bf16[1024,384]{1,0:T(8,128)(2,1)}, u32[]{:S(2)}, u32[]{:S(2)}) collective-permute-start(bf16[1024,384]{1,0:T(8,128)(2,1)} %convolution_convert_fusion.4), channel_id=1, source_target_pairs={{0,1},{1,0},{2,3},{3,2},{4,5},{5,4},{6,7},{7,6},{8,9},{9,8},{10,11... | collective-permute-start | bytes 2359304 | tf_op jit(solution)/shard_map/ppermute | solution.py:399
  155.9 9.3 %all-to-all-start = ((bf16[8,128,2]{1,2,0:T(2,128)(2,1)}), bf16[8,128,2]{1,2,0:T(2,128)(2,1)S(1)}, u32[]{:S(2)}, u32[]{:S(2)}) async-start(bf16[8,128,2]{1,2,0:T(2,128)(2,1)} %copy.25), calls=%async_computation.1 | async-start | bytes 8192 | tf_op jit(solution)/shard_map/all_to_all | solution.py:418
  159.6 68.7 %collective-permute-start.1 = (bf16[1024,384]{1,0:T(8,128)(2,1)S(1)}, bf16[1024,384]{1,0:T(8,128)(2,1)}, u32[]{:S(2)}, u32[]{:S(2)}) collective-permute-start(bf16[1024,384]{1,0:T(8,128)(2,1)S(1)} %copy-done.17), channel_id=1, source_target_pairs={{0,1},{1,0},{2,3},{3,2},{4,5},{5,4},{6,7},{7,6},{8,9},{9,8},{10,11... | collective-permute-start | bytes 2359304 | tf_op jit(solution)/shard_map/ppermute | solution.py:397
  160.5 64.0 %collective-permute-start.3 = (bf16[1024,384]{1,0:T(8,128)(2,1)}, bf16[1024,384]{1,0:T(8,128)(2,1)}, u32[]{:S(2)}, u32[]{:S(2)}) collective-permute-start(bf16[1024,384]{1,0:T(8,128)(2,1)} %convolution_convert_fusion.5), channel_id=1, source_target_pairs={{0,1},{1,0},{2,3},{3,2},{4,5},{5,4},{6,7},{7,6},{8,9},{9,8},{10,11... | collective-permute-start | bytes 2359304 | tf_op jit(solution)/shard_map/ppermute | solution.py:399
  161.7 78.9 %collective-permute-start.2 = (bf16[1024,384]{1,0:T(8,128)(2,1)S(1)}, bf16[1024,384]{1,0:T(8,128)(2,1)}, u32[]{:S(2)}, u32[]{:S(2)}) collective-permute-start(bf16[1024,384]{1,0:T(8,128)(2,1)S(1)} %copy-done.16), channel_id=1, source_target_pairs={{0,1},{1,0},{2,3},{3,2},{4,5},{5,4},{6,7},{7,6},{8,9},{9,8},{10,11... | collective-permute-start | bytes 2359304 | tf_op jit(solution)/shard_map/ppermute | solution.py:397
  165.8 11.2 %copy-start.14 = (bf16[1024,2048]{1,0:T(8,128)(2,1)S(1)}, bf16[1024,2048]{1,0:T(8,128)(2,1)}, u32[]{:S(2)}) copy-start(bf16[1024,2048]{1,0:T(8,128)(2,1)} %get-tuple-element.28) | copy-start | bytes 12582916
  165.8 11.2 %copy-start.20 = (bf16[1024,384]{0,1:T(8,128)(2,1)S(1)}, bf16[1024,384]{0,1:T(8,128)(2,1)}, u32[]{:S(2)}) copy-start(bf16[1024,384]{0,1:T(8,128)(2,1)} %copy-done.19) | copy-start | bytes 2359300
  177.0 13.8 %copy-start.9 = (bf16[1024,384]{0,1:T(8,128)(2,1)S(1)}, bf16[1024,384]{0,1:T(8,128)(2,1)}, u32[]{:S(2)}) copy-start(bf16[1024,384]{0,1:T(8,128)(2,1)} %copy-done.8) | copy-start | bytes 2359300
  177.0 13.8 %copy-start.12 = (bf16[1024,2048]{1,0:T(8,128)(2,1)S(1)}, bf16[1024,2048]{1,0:T(8,128)(2,1)}, u32[]{:S(2)}) copy-start(bf16[1024,2048]{1,0:T(8,128)(2,1)} %get-tuple-element.25) | copy-start | bytes 12582916
  193.6 30.9 %copy-start.7 = (bf16[1024,384]{0,1:T(8,128)(2,1)S(1)}, bf16[1024,384]{0,1:T(8,128)(2,1)}, u32[]{:S(2)}) copy-start(bf16[1024,384]{0,1:T(8,128)(2,1)} %copy-done.6) | copy-start | bytes 2359300
  226.9 1.3 copy-start.5
  228.3 12.3 %copy-start.3 = (bf16[1024,384]{0,1:T(8,128)(2,1)S(1)}, bf16[1024,384]{0,1:T(8,128)(2,1)}, u32[]{:S(2)}) copy-start(bf16[1024,384]{0,1:T(8,128)(2,1)} %copy-done.2) | copy-start | bytes 2359300
Sparse Core Ops, SparseCore 0:
  153.3 49.5 reduce-scatter.1
